TPU v7x, 32 devices: a whole 2x2x4 slice. The times are simulated.
32 devices in a mesh: section: 2 (over y), dp: 16 (over z, x, core).
Axes of the slice: x: 2, y: 2, z: 4, core: 2. Of those that a mesh axis runs over, the one named last changes fastest.
Arguments:
- inputs: bfloat16 [2, 2, 16, 1024, 512], P('section', None, 'dp'), may hold values from -6 to 6
- positions: float32 [2, 1024, 512], P('section', None, 'dp'), may hold values from -6 to 6
- projections: float32 [2, 4, 512, 512], P('section', None, 'dp'), may hold values from -0.25 to 0.25
- out_projections: float32 [2, 2, 512, 512], P('section', None, 'dp'), may hold values from -0.75 to 0.75
- ffn_up: float32 [2, 512, 2048], P('section', 'dp'), may hold values from -0.25 to 0.25
- ffn_down: float32 [2, 2048, 512], P('section', 'dp'), may hold values from -0.125 to 0.125
- norm_gains: float32 [2, 3, 512], P('section', None, 'dp'), may hold values from 0.5 to 1.5
- segments: int32 [2, 16, 1024], P(None, 'dp'), may hold values from 0 to 31, never falling along the last dimension, each value on 1 to 64 neighbouring positions
- levels: int32 [2, 2, 16, 1024], P(None, None, 'dp'), may hold values from 0 to 7
- cotangent: bfloat16 [2, 16, 1024, 512], P(None, 'dp'), may hold values from -6 to 6
Outputs:
- section_outputs: bfloat16 [2, 2, 16, 1024, 512], P('section', None, 'dp')
- grad_inputs: float32 [2, 2, 16, 1024, 512], P('section', None, 'dp')
- grad_positions: float32 [2, 1024, 512], P('section', None, 'dp')
- grad_projections: float32 [2, 4, 512, 512], P('section', None, 'dp')
- grad_out_projections: float32 [2, 2, 512, 512], P('section', None, 'dp')
- grad_ffn_up: float32 [2, 512, 2048], P('section', 'dp')
- grad_ffn_down: float32 [2, 2048, 512], P('section', 'dp')
- grad_norm_gains: float32 [2, 3, 512], P('section', None, 'dp')
Inputs may be any that keep to these rules, and one draw needn't show every extreme that they name: `segments`: in each row of 1024 positions the ids never fall, and each sentence holds 1 to 64 positions. levels[0] is 0 at padded source positions.
All inputs are finite; a program needn't handle non-finite values.
Results may differ from a plain program's by a relative error of at most 0.02.
The roundings to bfloat16 on the way count: a program that leaves them out, or rounds other values in their place, can miss the bound.
Values may be sent and summed in bfloat16 or wider, within the bound.
A program may use at most 704 MiB of HBM per device.

v0:
```python
from functools import partial

import jax
import jax.numpy as jnp
from jax import lax
from jax.sharding import PartitionSpec as P

H = 8
DH = 64
MB = 2


def from_behind(shard, axis, by):
    size = lax.axis_size(axis)
    pairs = [(i, i + by) for i in range(size) if 0 <= i + by < size]
    return lax.ppermute(shard, axis, pairs)


def section_tools():

    def low(v):
        return lax.optimization_barrier(v.astype(jnp.bfloat16)).astype(jnp.float32)

    def low_back(v):
        return v

    low = jax.custom_vjp(low)
    low_back = jax.custom_vjp(low_back)

    def low_keep(v):
        return (low(v), None)

    def low_pass(kept, grad):
        return (grad,)

    def back_keep(v):
        return (v, None)

    def back_low(kept, grad):
        return (low(grad),)

    low.defvjp(low_keep, low_pass)
    low_back.defvjp(back_keep, back_low)

    def rounded(value):
        return low(low_back(value))

    def product(left, right):
        return jnp.dot(
            left.astype(jnp.bfloat16),
            right.astype(jnp.bfloat16),
            preferred_element_type=jnp.float32,
        )

    product = jax.custom_vjp(product)

    def product_keep(left, right):
        return (product(left, right), (left.astype(jnp.bfloat16), right.astype(jnp.bfloat16)))

    def product_back(kept, grad):
        left, right = kept
        grad_low = grad.astype(jnp.bfloat16)
        left_grad = lax.dot_general(
            grad_low, right, (((1,), (1,)), ((), ())), preferred_element_type=jnp.float32
        )
        right_grad = lax.dot_general(
            left, grad_low, (((0,), (0,)), ((), ())), preferred_element_type=jnp.float32
        )
        return (left_grad, right_grad)

    product.defvjp(product_keep, product_back)

    def layer_norm(stream, gain_vector):
        average = jnp.mean(stream, axis=-1, keepdims=True)
        centred = stream - average
        variance = jnp.mean(centred * centred, axis=-1, keepdims=True)
        return gain_vector * centred * lax.rsqrt(variance + 1e-05)

    def feed(stream, gain_vector, up_weight, down_weight):
        normed = low(layer_norm(stream, gain_vector))
        hidden = low(jax.nn.gelu(low_back(product(normed, up_weight)), approximate=False))
        return low_back(product(hidden, down_weight))

    def window_of(length, block_rows, offset):
        margin = length // 16
        window = min(length, block_rows + 2 * margin)
        start = jnp.clip(offset - margin, 0, length - window)
        return (start, window)

    def code_mask(seg_block, key_segments, code_block, key_codes, offset, start, diagonal):
        visible = key_codes[None, :] < code_block[:, None]
        if diagonal:
            row_ids = offset + lax.iota(jnp.int32, seg_block.shape[0])
            col_ids = start + lax.iota(jnp.int32, key_segments.shape[0])
            visible = visible | (row_ids[:, None] == col_ids[None, :])
        return (seg_block[:, None] == key_segments[None, :]) & visible

    def block_scores(
        query_block,
        key_heads,
        seg_block,
        key_segments,
        code_block,
        key_codes,
        offset,
        start,
        diagonal,
    ):
        scores = jnp.einsum(
            "qhd,khd->hqk", query_block, key_heads, preferred_element_type=jnp.float32
        ) * DH ** (-0.5)
        allowed = code_mask(seg_block, key_segments, code_block, key_codes, offset, start, diagonal)
        return jnp.where(allowed[None], scores, -1e30)

    def block_inputs(
        queries,
        key_heads,
        value_heads,
        query_segments,
        key_segments,
        query_codes,
        key_codes,
        offset,
        block_rows,
        length,
    ):
        start, window = window_of(length, block_rows, offset)
        query_block = lax.dynamic_slice_in_dim(queries, offset, block_rows, 0).reshape(
            block_rows, H, DH
        )
        seg_block = lax.dynamic_slice_in_dim(query_segments, offset, block_rows, 0)
        code_block = lax.dynamic_slice_in_dim(query_codes, offset, block_rows, 0)
        key_part = lax.dynamic_slice_in_dim(key_heads, start, window, 0)
        value_part = lax.dynamic_slice_in_dim(value_heads, start, window, 0)
        key_seg_part = lax.dynamic_slice_in_dim(key_segments, start, window, 0)
        key_code_part = lax.dynamic_slice_in_dim(key_codes, start, window, 0)
        return (
            start,
            window,
            query_block,
            seg_block,
            code_block,
            key_part,
            value_part,
            key_seg_part,
            key_code_part,
        )

    def attention_rows(packed, diagonal):
        queries, key_rows, value_rows, query_segments, key_segments, query_codes, key_codes = packed
        length = queries.shape[0]
        block_rows = min(512, length)
        blocks = length // block_rows
        key_heads = key_rows.reshape(length, H, DH)
        value_heads = value_rows.reshape(length, H, DH)

        def one_block(block_index):
            offset = block_index * block_rows
            (
                start,
                window,
                query_block,
                seg_block,
                code_block,
                key_part,
                value_part,
                key_seg_part,
                key_code_part,
            ) = block_inputs(
                queries,
                key_heads,
                value_heads,
                query_segments,
                key_segments,
                query_codes,
                key_codes,
                offset,
                block_rows,
                length,
            )
            scores = block_scores(
                query_block,
                key_part,
                seg_block,
                key_seg_part,
                code_block,
                key_code_part,
                offset,
                start,
                diagonal,
            )
            row_max = jnp.max(scores, axis=-1, keepdims=True)
            shifted = jnp.exp(scores - row_max)
            row_sum = jnp.sum(shifted, axis=-1, keepdims=True)
            weights = (shifted / row_sum).astype(jnp.bfloat16)
            mixed_heads = jnp.einsum(
                "hqk,khd->qhd", weights, value_part, preferred_element_type=jnp.float32
            )
            return (mixed_heads.reshape(block_rows, H * DH), (row_max + jnp.log(row_sum))[..., 0])

        mixed_rows, row_lse = lax.map(one_block, jnp.arange(blocks))
        return (mixed_rows.reshape(length, H * DH), row_lse)

    def attention_rows_back(packed, diagonal):
        (
            queries,
            key_rows,
            value_rows,
            query_segments,
            key_segments,
            query_codes,
            key_codes,
            row_lse,
            d_mixed,
        ) = packed
        length = queries.shape[0]
        block_rows = min(512, length)
        blocks = length // block_rows
        key_heads = key_rows.reshape(length, H, DH)
        value_heads = value_rows.reshape(length, H, DH)

        def one_block(running, block_index):
            d_keys, d_values = running
            offset = block_index * block_rows
            (
                start,
                window,
                query_block,
                seg_block,
                code_block,
                key_part,
                value_part,
                key_seg_part,
                key_code_part,
            ) = block_inputs(
                queries,
                key_heads,
                value_heads,
                query_segments,
                key_segments,
                query_codes,
                key_codes,
                offset,
                block_rows,
                length,
            )
            grad_block = (
                lax.dynamic_slice_in_dim(d_mixed, offset, block_rows, 0)
                .astype(jnp.bfloat16)
                .reshape(block_rows, H, DH)
            )
            scores = block_scores(
                query_block,
                key_part,
                seg_block,
                key_seg_part,
                code_block,
                key_code_part,
                offset,
                start,
                diagonal,
            )
            weights = jnp.exp(scores - row_lse[block_index][..., None])
            d_weights = jnp.einsum(
                "qhd,khd->hqk", grad_block, value_part, preferred_element_type=jnp.float32
            )
            d_scores = (
                weights * (d_weights - jnp.sum(weights * d_weights, axis=-1, keepdims=True))
            ).astype(jnp.bfloat16)
            value_term = jnp.einsum(
                "hqk,qhd->khd",
                weights.astype(jnp.bfloat16),
                grad_block,
                preferred_element_type=jnp.float32,
            )
            key_term = jnp.einsum(
                "hqk,qhd->khd", d_scores, query_block, preferred_element_type=jnp.float32
            ) * DH ** (-0.5)
            d_values = lax.dynamic_update_slice_in_dim(
                d_values,
                lax.dynamic_slice_in_dim(d_values, start, window, 0) + value_term,
                start,
                0,
            )
            d_keys = lax.dynamic_update_slice_in_dim(
                d_keys, lax.dynamic_slice_in_dim(d_keys, start, window, 0) + key_term, start, 0
            )
            d_query = jnp.einsum(
                "hqk,khd->qhd", d_scores, key_part, preferred_element_type=jnp.float32
            ) * DH ** (-0.5)
            return ((d_keys, d_values), d_query.reshape(block_rows, H * DH))

        empty_heads = jnp.zeros((length, H, DH), jnp.float32)
        (d_keys, d_values), d_queries = lax.scan(
            one_block, (empty_heads, empty_heads), jnp.arange(blocks)
        )
        return (
            d_queries.reshape(length, H * DH),
            d_keys.reshape(length, H * DH),
            d_values.reshape(length, H * DH),
        )

    def attention_keep(
        queries,
        key_rows,
        value_rows,
        query_segments,
        key_segments,
        query_codes,
        key_codes,
        diagonal,
    ):
        packed = (
            queries.astype(jnp.bfloat16),
            key_rows.astype(jnp.bfloat16),
            value_rows.astype(jnp.bfloat16),
            query_segments,
            key_segments,
            query_codes,
            key_codes,
        )
        mixed_rows, row_lse = lax.map(partial(attention_rows, diagonal=diagonal), packed)
        return (mixed_rows, (packed, row_lse))

    def attention(
        queries,
        key_rows,
        value_rows,
        query_segments,
        key_segments,
        query_codes,
        key_codes,
        diagonal,
    ):
        return attention_keep(
            queries,
            key_rows,
            value_rows,
            query_segments,
            key_segments,
            query_codes,
            key_codes,
            diagonal,
        )[0]

    attention = jax.custom_vjp(attention, nondiff_argnums=(7,))

    def attention_back(diagonal, kept, d_mixed):
        packed, row_lse = kept
        d_queries, d_keys, d_values = lax.map(
            partial(attention_rows_back, diagonal=diagonal), packed + (row_lse, d_mixed)
        )
        return (d_queries, d_keys, d_values, None, None, None, None)

    attention.defvjp(attention_keep, attention_back)

    def as_rows(value, batch):
        return value.reshape(batch, -1, value.shape[-1])

    def usable_codes(segment_rows, level_row):
        starts = jnp.concatenate(
            [
                jnp.ones(segment_rows.shape[:-1] + (1,), bool),
                segment_rows[:, 1:] != segment_rows[:, :-1],
            ],
            axis=1,
        )
        return jnp.where((level_row > 0) | starts, 0, 2).astype(jnp.int32)

    def spare_section(weights, own, kv_pair, segment_rows, level_rows):
        empty = jnp.zeros_like(own)
        return (empty, empty, empty)

    def encode_section(weights, own, kv_pair, segment_rows, level_rows):
        inner, outer, up_weight, down_weight, gain_rows, table = weights
        batch, length, width = own.shape
        stream = (own + table[None]).reshape(batch * length, width)
        normed = low(layer_norm(stream, gain_rows[0]))
        queries = as_rows(rounded(product(normed, inner[0])), batch)
        key_rows = as_rows(rounded(product(normed, inner[1])), batch)
        value_rows = as_rows(rounded(product(normed, inner[2])), batch)
        key_codes = usable_codes(segment_rows, level_rows[0])
        query_codes = jnp.ones_like(segment_rows)
        mixed_rows = rounded(
            attention(
                queries,
                key_rows,
                value_rows,
                segment_rows,
                segment_rows,
                query_codes,
                key_codes,
                False,
            )
        )
        stream = stream + low_back(product(mixed_rows.reshape(batch * length, width), outer[0]))
        stream = stream + feed(stream, gain_rows[1], up_weight, down_weight)
        memory = low(layer_norm(stream, gain_rows[2]))
        cross_keys = rounded(product(memory, inner[3]))
        cross_values = rounded(product(memory, outer[1]))
        return (as_rows(memory, batch), as_rows(cross_keys, batch), as_rows(cross_values, batch))

    def decode_section(weights, own, kv_pair, segment_rows, level_rows):
        inner, outer, up_weight, down_weight, gain_rows, table = weights
        batch, length, width = own.shape
        embedded = (own + table[None]).reshape(batch * length, width)
        stream = jnp.broadcast_to(table[None], own.shape).reshape(batch * length, width)
        normed = low(layer_norm(stream, gain_rows[0]))
        normed_keys = low(layer_norm(embedded, gain_rows[0]))
        queries = as_rows(rounded(product(normed, inner[0])), batch)
        key_rows = as_rows(rounded(product(normed_keys, inner[1])), batch)
        value_rows = as_rows(rounded(product(normed_keys, inner[2])), batch)
        target_codes = level_rows[1]
        mixed_rows = rounded(
            attention(
                queries,
                key_rows,
                value_rows,
                segment_rows,
                segment_rows,
                target_codes,
                target_codes,
                True,
            )
        )
        stream = stream + low_back(product(mixed_rows.reshape(batch * length, width), outer[0]))
        normed_cross = low(layer_norm(stream, gain_rows[1]))
        cross_queries = as_rows(rounded(product(normed_cross, inner[3])), batch)
        source_codes = usable_codes(segment_rows, level_rows[0])
        mixed_cross = rounded(
            attention(
                cross_queries,
                kv_pair[0],
                kv_pair[1],
                segment_rows,
                segment_rows,
                jnp.ones_like(segment_rows),
                source_codes,
                False,
            )
        )
        stream = stream + low_back(product(mixed_cross.reshape(batch * length, width), outer[1]))
        stream = stream + feed(stream, gain_rows[2], up_weight, down_weight)
        empty = jnp.zeros_like(own)
        return (as_rows(stream, batch), empty, empty)

    def run_section(branch, segment_rows, level_rows, weights, own, kv_pair):
        return lax.switch(
            branch,
            [spare_section, encode_section, decode_section],
            weights,
            own,
            kv_pair,
            segment_rows,
            level_rows,
        )

    return run_section


def body(
    inputs,
    positions,
    projections,
    out_projections,
    ffn_up,
    ffn_down,
    norm_gains,
    segments,
    levels,
    cotangent,
):
    run_section = section_tools()
    section_index = lax.axis_index("section")
    gathered = (
        lax.all_gather(projections.astype(jnp.bfloat16), "dp", axis=2, tiled=True),
        lax.all_gather(out_projections.astype(jnp.bfloat16), "dp", axis=2, tiled=True),
        lax.all_gather(ffn_up.astype(jnp.bfloat16), "dp", axis=1, tiled=True),
        lax.all_gather(ffn_down.astype(jnp.bfloat16), "dp", axis=1, tiled=True),
        lax.all_gather(norm_gains.astype(jnp.bfloat16), "dp", axis=2, tiled=True),
        lax.all_gather(positions.astype(jnp.bfloat16), "dp", axis=2, tiled=True),
    )
    weights = tuple((piece[0].astype(jnp.float32) for piece in gathered))
    own_inputs = inputs[0]
    empty_rows = jnp.zeros(own_inputs.shape[1:], jnp.bfloat16)
    received = (empty_rows, empty_rows)
    pullbacks = []
    outputs = jnp.zeros(own_inputs.shape, jnp.bfloat16)
    for tick in range(MB + 1):
        micro_index = tick - section_index
        valid = (micro_index >= 0) & (micro_index < MB)
        clipped = jnp.clip(micro_index, 0, MB - 1)
        branch = jnp.where(valid, 1 + section_index, 0)
        own = lax.dynamic_index_in_dim(own_inputs, clipped, 0, keepdims=False).astype(jnp.float32)
        segment_rows = lax.dynamic_index_in_dim(segments, clipped, 0, keepdims=False)
        level_rows = lax.dynamic_index_in_dim(levels, clipped, 1, keepdims=False)
        kv_pair = (received[0].astype(jnp.float32), received[1].astype(jnp.float32))
        result, pullback = jax.vjp(
            partial(run_section, branch, segment_rows, level_rows), weights, own, kv_pair
        )
        pullbacks.append(pullback)
        main_rows, sent_keys, sent_values = result
        outputs = jnp.where(
            valid,
            lax.dynamic_update_index_in_dim(outputs, main_rows.astype(jnp.bfloat16), clipped, 0),
            outputs,
        )
        if tick < MB:
            received = from_behind(
                (sent_keys.astype(jnp.bfloat16), sent_values.astype(jnp.bfloat16)), "section", 1
            )
    is_decoder = section_index == 1
    grads_in = jnp.zeros(own_inputs.shape, jnp.float32)
    returned = (empty_rows, empty_rows)
    summed = None
    for back_step in range(MB + 1):
        tick = MB - back_step
        micro_index = tick - section_index
        valid = (micro_index >= 0) & (micro_index < MB)
        clipped = jnp.clip(micro_index, 0, MB - 1)
        own_grad = lax.dynamic_index_in_dim(cotangent, clipped, 0, keepdims=False).astype(
            jnp.float32
        )
        own_grad = jnp.where(valid & is_decoder, own_grad, 0.0)
        d_weights, d_own, d_kv = pullbacks[tick](
            (own_grad, returned[0].astype(jnp.float32), returned[1].astype(jnp.float32))
        )
        grads_in = jnp.where(
            valid, lax.dynamic_update_index_in_dim(grads_in, d_own, clipped, 0), grads_in
        )
        if back_step < MB:
            returned = from_behind(
                (d_kv[0].astype(jnp.bfloat16), d_kv[1].astype(jnp.bfloat16)), "section", -1
            )
        summed = (
            d_weights
            if summed is None
            else tuple(
                (first_term + second_term for first_term, second_term in zip(summed, d_weights))
            )
        )
    summed = (
        lax.psum_scatter(summed[0], "dp", scatter_dimension=1, tiled=True),
        lax.psum_scatter(summed[1], "dp", scatter_dimension=1, tiled=True),
        lax.psum_scatter(summed[2], "dp", scatter_dimension=0, tiled=True),
        lax.psum_scatter(summed[3], "dp", scatter_dimension=0, tiled=True),
        lax.psum_scatter(summed[4], "dp", scatter_dimension=1, tiled=True),
        lax.psum_scatter(summed[5], "dp", scatter_dimension=1, tiled=True),
    )
    return (
        outputs[None],
        grads_in[None],
        summed[5][None],
        summed[0][None],
        summed[1][None],
        summed[2][None],
        summed[3][None],
        summed[4][None],
    )


def solution(mesh):
    in_specs = (
        P("section", None, "dp", None, None),
        P("section", None, "dp"),
        P("section", None, "dp", None),
        P("section", None, "dp", None),
        P("section", "dp", None),
        P("section", "dp", None),
        P("section", None, "dp"),
        P(None, "dp", None),
        P(None, None, "dp", None),
        P(None, "dp", None, None),
    )
    out_specs = (
        P("section", None, "dp", None, None),
        P("section", None, "dp", None, None),
        P("section", None, "dp"),
        P("section", None, "dp", None),
        P("section", None, "dp", None),
        P("section", "dp", None),
        P("section", "dp", None),
        P("section", None, "dp"),
    )
    return jax.shard_map(body, mesh=mesh, in_specs=in_specs, out_specs=out_specs, check_vma=False)
```

profile of v0, /device:TPU:0, one launch (start us, length us, event | category | flops | bytes accessed | tf_op | source)
XLA Modules:
  0.0 2234.9 jit_solution(11968379208140435003)
XLA Ops:
  16.5 23.8 %all_gather.18 = bf16[1,3,512]{1,0,2:T(2,128)(2,1)S(1)} all-gather(bf16[1,3,32]{1,0,2:T(2,128)(2,1)S(1)} %copy.671), channel_id=1, replica_groups=mesh['section'=2,'dp'=16] {'dp'}, dimensions={2}, use_global_device_ids=true | all-gather | bytes 3264 | tf_op jit(solution)/shard_map/all_gather | solution.py:480
  53.0 38.2 %all-gather.10.cloned.1.call-done = bf16[1,2,512,512]{3,2,1,0:T(8,128)(2,1)} async-done(((bf16[1,2,32,512]{3,2,1,0:T(8,128)(2,1)}), bf16[1,2,512,512]{3,2,1,0:T(8,128)(2,1)}) %all-gather.10.cloned.1.call-update) | async-done | bytes 1048592 | tf_op jit(solution)/shard_map/all_gather | solution.py:477
  91.2 43.1 %all-gather.8.cloned.1.call-done = bf16[1,4,512,512]{3,2,1,0:T(8,128)(2,1)} async-done(((bf16[1,4,32,512]{3,2,1,0:T(8,128)(2,1)}), bf16[1,4,512,512]{3,2,1,0:T(8,128)(2,1)}) %all-gather.8.cloned.1.call-update) | async-done | bytes 2097168 | tf_op jit(solution)/shard_map/all_gather | solution.py:476
  134.3 42.8 %all-gather.12.cloned.1.call-done = bf16[1,512,2048]{2,1,0:T(8,128)(2,1)} async-done(((bf16[1,32,2048]{2,1,0:T(8,128)(2,1)}), bf16[1,512,2048]{2,1,0:T(8,128)(2,1)}) %all-gather.12.cloned.1.call-update) | async-done | bytes 2097168 | tf_op jit(solution)/shard_map/all_gather | solution.py:478
  177.1 42.8 %all-gather.14.cloned.1.call-done = bf16[1,2048,512]{2,1,0:T(8,128)(2,1)} async-done(((bf16[1,128,512]{2,1,0:T(8,128)(2,1)}), bf16[1,2048,512]{2,1,0:T(8,128)(2,1)}) %all-gather.14.cloned.1.call-update) | async-done | bytes 2097168 | tf_op jit(solution)/shard_map/all_gather | solution.py:479
  221.0 139.0 %conditional.6 = (bf16[1,1024,512]{2,1,0:T(8,128)(2,1)}, bf16[1,1024,512]{2,1,0:T(8,128)(2,1)}, f32[1024,512]{0,1:T(8,128)}, f32[1,512]{1,0:T(1,128)}, f32[1024,...) conditional(s32[]{:T(128)} %clamp.9, () %tuple.491, ...), branch_computations={%region_0.1_spmd.clone, %region_1.12_spmd.clone, %region_12.29_spm... | conditional | flops 9079830528 | bytes 292424704 | solution.py:448
  243.9 32.2 %while.494 = (s32[]{:T(128)}, bf16[2,512,512]{1,2,0:T(8,128)(2,1)}, f32[2,8,512]{2,1,0:T(8,128)S(1)}, s32[2]{0:T(128)S(1)}, bf16[1024,8,64]{0,2,1:T(8,128)(2,1)}...) while((s32[]{:T(128)}, bf16[2,512,512]{1,2,0:T(8,128)(2,1)}, ...), condition=%wide.region_7.7_spmd, body=%wide.region_4.6_spmd.sunk | while | flops 703197824 | bytes 51005032 | solution.py:385
  287.0 23.3 %multiply_convert_fusion.30 = (bf16[1024,2048]{1,0:T(8,128)(2,1)}, f32[1024,2048]{1,0:T(8,128)}, f32[1024,2048]{1,0:T(8,128)}, f32[1024,2048]{1,0:T(8,128)}) fusion(bf16[1024,512]{0,1:T(8,128)(2,1)} %get-tuple-element.10048, bf16[512,2048]{1,0:T(8,128)(2,1)S(1)} %copy-done.14), kind=kOutput, calls=%fused_computation.950 | convolution fusion | flops 2283798528 | bytes 32505856 | tf_op jit(solution)/shard_map/jvp()/cond/branch_1_fun/dot_general | solution.py:81
  374.3 13.1 collective-permute-done
  387.4 22.1 collective-permute-done.1
  409.5 145.1 %conditional.7 = (bf16[1,1024,512]{2,1,0:T(8,128)(2,1)}, bf16[1,1024,512]{2,1,0:T(8,128)(2,1)}, f32[1024,512]{0,1:T(8,128)}, f32[1,512]{1,0:T(1,128)}, f32[1024,...) conditional(s32[]{:T(128)} %clamp.10, () %tuple.494, ...), branch_computations={%region_29.30_spmd, %region_30.41_spmd, %region_41.58_spmd} | conditional | flops 9079830528 | bytes 286108608 | solution.py:448
  434.9 32.2 %while.479 = (s32[]{:T(128)}, bf16[2,512,512]{1,2,0:T(8,128)(2,1)}, f32[2,8,512]{2,1,0:T(8,128)S(1)}, s32[2]{0:T(128)S(1)}, bf16[1024,8,64]{0,2,1:T(8,128)(2,1)}...) while((s32[]{:T(128)}, bf16[2,512,512]{1,2,0:T(8,128)(2,1)}, ...), condition=%wide.region_36.36_spmd, body=%wide.region_33.35_spmd.sunk | while | flops 703197824 | bytes 51005032 | solution.py:385
  477.9 23.7 %multiply_convert_fusion.12 = (bf16[1024,2048]{1,0:T(8,128)(2,1)}, f32[1024,2048]{1,0:T(8,128)}, f32[1024,2048]{1,0:T(8,128)}, f32[1024,2048]{1,0:T(8,128)}) fusion(bf16[1024,512]{0,1:T(8,128)(2,1)} %get-tuple-element.9940, bf16[512,2048]{1,0:T(8,128)(2,1)S(1)} %copy-done.17), kind=kOutput, calls=%fused_computation.670 | convolution fusion | flops 2283798528 | bytes 32505856 | tf_op jit(solution)/shard_map/jvp()/cond/branch_1_fun/dot_general | solution.py:81
  557.0 27.8 %collective-permute-start.2 = (bf16[1,1024,512]{1,2,0:T(8,128)(2,1)}, bf16[1,1024,512]{1,2,0:T(8,128)(2,1)}, u32[]{:S(2)}, u32[]{:S(2)}) collective-permute-start(bf16[1,1024,512]{1,2,0:T(8,128)(2,1)} %copy.684), channel_id=1, source_target_pairs={{0,16},{1,17},{2,18},{3,19},{4,20},{5,21},{6,22},{7,23},{8,24},{9,... | collective-permute-start | bytes 3145736 | tf_op jit(solution)/shard_map/ppermute | solution.py:16
  595.7 11.9 collective-permute-done.2
  607.6 21.3 collective-permute-done.3
  628.9 70.6 %conditional.8 = (f32[1024,512]{0,1:T(8,128)}, f32[1,512]{1,0:T(1,128)}, f32[1024,1]{0,1:T(1,128)}, f32[1024,1]{0,1:T(1,128)}, f32[1024,512]{0,1:T(8,128)}, /*in...) conditional(s32[]{:T(128)} %clamp.11, () %tuple.497, ...), branch_computations={%region_58.59_spmd, %region_59.70_spmd, %region_70.87_spmd} | conditional | flops 9079830528 | bytes 284044256 | solution.py:448
  699.5 25.9 %conditional.9 = (f32[2048,512]{1,0:T(8,128)}, f32[3,512]{1,0:T(4,128)}, f32[1024,512]{0,1:T(8,128)}, f32[1,1024,512]{1,2,0:T(8,128)}, f32[1,1024,512]{1,2,0:T(8...) conditional(s32[]{:T(128)} %clamp.11, () %tuple.500, ...), branch_computations={%region_87.88_spmd, %region_88.101_spmd, %region_101.120_spmd} | conditional | flops 18531356672 | bytes 686767232 | solution.py:448
  733.3 438.6 %collective-permute-done.4 = bf16[1,1024,512]{2,1,0:T(8,128)(2,1)} collective-permute-done((bf16[1,1024,512]{2,1,0:T(8,128)(2,1)}, bf16[1,1024,512]{2,1,0:T(8,128)(2,1)}, u32[]{:S(2)}, u32[]{:S(2)}) %collective-permute-start.4) | collective-permute-done | bytes 1048608 | tf_op jit(solution)/shard_map/ppermute | solution.py:16
  1171.9 20.5 collective-permute-done.5
  1192.4 228.8 %conditional.10 = (f32[2048,512]{1,0:T(8,128)}, f32[3,512]{1,0:T(4,128)}, f32[1024,512]{0,1:T(8,128)}, f32[1,1024,512]{1,2,0:T(8,128)}, f32[1,1024,512]{1,2,0:T(...) conditional(s32[]{:T(128)} %clamp.10, () %tuple.503, ...), branch_computations={%region_120.121_spmd, %region_121.134_spmd, %region_134.153_spmd} | conditional | flops 18531356672 | bytes 682564736 | solution.py:448
  1254.8 104.3 %while.488 = (s32[]{:T(128)}, f32[1024,8,64]{0,2,1:T(8,128)}, f32[1024,8,64]{0,2,1:T(8,128)}, bf16[2,512,512]{2,1,0:T(8,128)(2,1)}, s32[2]{0:T(128)S(1)}, /*inde...) while((s32[]{:T(128)}, f32[1024,8,64]{0,2,1:T(8,128)}, ...), condition=%wide.region_128.128_spmd, body=%wide.region_126.127_spmd.sunk | while | flops 1719529472 | bytes 173813360 | solution.py:385
  1429.1 134.9 %collective-permute-done.6 = bf16[1,1024,512]{2,1,0:T(8,128)(2,1)S(1)} collective-permute-done((bf16[1,1024,512]{2,1,0:T(8,128)(2,1)}, bf16[1,1024,512]{2,1,0:T(8,128)(2,1)S(1)}, u32[]{:S(2)}, u32[]{:S(2)}) %collective-permute-start.6) | collective-permute-done | bytes 1048608 | tf_op jit(solution)/shard_map/ppermute | solution.py:16
  1564.0 20.0 collective-permute-done.7
  1584.0 230.2 %conditional.11 = (f32[2048,512]{1,0:T(8,128)}, f32[3,512]{1,0:T(4,128)}, f32[1024,512]{0,1:T(8,128)}, f32[1,1,1024,512]{3,2,1,0:T(8,128)}, f32[4,512,512]{2,1,0...) conditional(s32[]{:T(128)} %clamp.9, () %tuple.506, ...), branch_computations={%region_153.154_spmd, %region_154.167_spmd, %region_167.186_spmd} | conditional | flops 17848799232 | bytes 615103552 | solution.py:448
  1616.5 12.7 add_convert_fusion.6
  1649.7 103.0 %while.491 = (s32[]{:T(128)}, f32[1024,8,64]{0,2,1:T(8,128)}, f32[1024,8,64]{0,2,1:T(8,128)}, bf16[2,512,512]{2,1,0:T(8,128)(2,1)}, s32[2]{0:T(128)S(1)}, /*inde...) while((s32[]{:T(128)}, f32[1024,8,64]{0,2,1:T(8,128)}, ...), condition=%wide.region_161.161_spmd, body=%wide.region_159.160_spmd.sunk | while | flops 1719529472 | bytes 173813360 | solution.py:385
  1870.4 63.6 %reduce-scatter.9.cloned.1.call-done = f32[1024,32]{0,1:T(8,128)} async-done(((f32[1024,512]{0,1:T(8,128)}), f32[1024,32]{0,1:T(8,128)}) %reduce-scatter.9.cloned.1.call-update) | async-done | bytes 131088 | tf_op jit(solution)/shard_map/reduce_scatter | solution.py:548
  1934.1 65.4 %reduce-scatter.13.cloned.1.call-done = f32[2,32,512]{2,1,0:T(8,128)} async-done(((f32[2,512,512]{2,1,0:T(8,128)}), f32[2,32,512]{2,1,0:T(8,128)}) %reduce-scatter.13.cloned.1.call-update) | async-done | bytes 131088 | tf_op jit(solution)/shard_map/reduce_scatter | solution.py:544
  1999.5 76.2 %reduce-scatter.11.cloned.1.call-done = f32[4,32,512]{2,1,0:T(8,128)} async-done(((f32[4,512,512]{2,1,0:T(8,128)}), f32[4,32,512]{2,1,0:T(8,128)}) %reduce-scatter.11.cloned.1.call-update) | async-done | bytes 262160 | tf_op jit(solution)/shard_map/reduce_scatter | solution.py:543
  2075.6 76.2 %reduce-scatter.15.cloned.1.call-done = f32[32,2048]{1,0:T(8,128)} async-done(((f32[512,2048]{1,0:T(8,128)}), f32[32,2048]{1,0:T(8,128)}) %reduce-scatter.15.cloned.1.call-update) | async-done | bytes 262160 | tf_op jit(solution)/shard_map/reduce_scatter | solution.py:545
  2151.9 76.0 %reduce-scatter.17.cloned.1.call-done = f32[128,512]{1,0:T(8,128)} async-done(((f32[2048,512]{1,0:T(8,128)}), f32[128,512]{1,0:T(8,128)}) %reduce-scatter.17.cloned.1.call-update) | async-done | bytes 262160 | tf_op jit(solution)/shard_map/reduce_scatter | solution.py:546
  (740 shorter events, 813.9 us)
Async XLA Ops:
  7.2 44.3 %all-gather.6.cloned.1.call-start = ((), (), s32[]{:S(2)}) async-start(), calls=%async_computation.6 | async-start | bytes 1114112 | tf_op jit(solution)/shard_map/all_gather | solution.py:481
  8.9 82.2 %all-gather.10.cloned.1.call-start = ((), (), s32[]{:S(2)}) async-start(), calls=%async_computation.8 | async-start | bytes 1114112 | tf_op jit(solution)/shard_map/all_gather | solution.py:477
  10.5 123.8 %all-gather.8.cloned.1.call-start = ((), (), s32[]{:S(2)}) async-start(), calls=%async_computation.7 | async-start | bytes 2228224 | tf_op jit(solution)/shard_map/all_gather | solution.py:476
  12.2 164.9 %all-gather.12.cloned.1.call-start = ((), (), s32[]{:S(2)}) async-start(), calls=%async_computation.9 | async-start | bytes 2228224 | tf_op jit(solution)/shard_map/all_gather | solution.py:478
  13.9 206.0 %all-gather.14.cloned.1.call-start = ((), (), s32[]{:S(2)}) async-start(), calls=%async_computation.10 | async-start | bytes 2228224 | tf_op jit(solution)/shard_map/all_gather | solution.py:479
  15.6 1853.4 %reduce-scatter.19.cloned.1.call-start = ((), (), s32[]{:S(2)}) async-start(), calls=%async_computation.16 | async-start | bytes 278528
  40.6 180.4 %copy-start.113 = (f32[1,3,512]{1,0,2:T(1,128)}, f32[1,3,512]{1,0,2:T(1,128)S(1)}, u32[]{:S(2)}) copy-start(f32[1,3,512]{1,0,2:T(1,128)S(1)} %convert_element_type.1933) | copy-start | bytes 18436
  226.6 56.7 %copy-start.279 = (f32[1,512]{1,0:T(1,128)}, f32[1,512]{1,0:T(1,128)S(1)}, u32[]{:S(2)}) copy-start(f32[1,512]{1,0:T(1,128)S(1)} %get-tuple-element.12589) | copy-start | bytes 6148 | tf_op jit(solution)/shard_map/jvp()/cond
  362.3 25.1 %collective-permute-start = (bf16[1,1024,512]{1,2,0:T(8,128)(2,1)}, bf16[1,1024,512]{1,2,0:T(8,128)(2,1)}, u32[]{:S(2)}, u32[]{:S(2)}) collective-permute-start(bf16[1,1024,512]{1,2,0:T(8,128)(2,1)} %copy.678), channel_id=1, source_target_pairs={{0,16},{1,17},{2,18},{3,19},{4,20},{5,21},{6,22},{7,23},{8,24},{9,... | collective-permute-start | bytes 3145736 | tf_op jit(solution)/shard_map/ppermute | solution.py:16
  366.8 42.7 %collective-permute-start.1 = (bf16[1,1024,512]{1,2,0:T(8,128)(2,1)}, bf16[1,1024,512]{1,2,0:T(8,128)(2,1)}, u32[]{:S(2)}, u32[]{:S(2)}) collective-permute-start(bf16[1,1024,512]{1,2,0:T(8,128)(2,1)} %copy.679), channel_id=1, source_target_pairs={{0,16},{1,17},{2,18},{3,19},{4,20},{5,21},{6,22},{7,23},{8,24},{9,... | collective-permute-start | bytes 3145736 | tf_op jit(solution)/shard_map/ppermute | solution.py:16
  369.1 40.4 %copy-start.68 = (bf16[1,2,512,512]{3,2,1,0:T(8,128)(2,1)S(1)}, bf16[1,2,512,512]{3,2,1,0:T(8,128)(2,1)}, u32[]{:S(2)}) copy-start(bf16[1,2,512,512]{3,2,1,0:T(8,128)(2,1)} %all-gather.10.cloned.1.call-done) | copy-start | bytes 3145732
  369.1 40.4 %copy-start.114 = (f32[1,3,512]{1,0,2:T(1,128)S(1)}, f32[1,3,512]{1,0,2:T(1,128)}, u32[]{:S(2)}) copy-start(f32[1,3,512]{1,0,2:T(1,128)} %copy-done.113) | copy-start | bytes 18436
  369.1 40.4 %copy-start.175 = (s32[1,1024]{1,0:T(1,128)S(1)}, s32[1,1024]{1,0:T(1,128)}, u32[]{:S(2)}) copy-start(s32[1,1024]{1,0:T(1,128)} %get-tuple-element.10345) | copy-start | bytes 12292
  415.1 59.1 %copy-start.275 = (f32[1,512]{1,0:T(1,128)}, f32[1,512]{1,0:T(1,128)S(1)}, u32[]{:S(2)}) copy-start(f32[1,512]{1,0:T(1,128)S(1)} %get-tuple-element.12746) | copy-start | bytes 6148 | tf_op jit(solution)/shard_map/jvp()/cond
  557.0 50.7 %collective-permute-start.2 = (bf16[1,1024,512]{1,2,0:T(8,128)(2,1)}, bf16[1,1024,512]{1,2,0:T(8,128)(2,1)}, u32[]{:S(2)}, u32[]{:S(2)}) collective-permute-start(bf16[1,1024,512]{1,2,0:T(8,128)(2,1)} %copy.684), channel_id=1, source_target_pairs={{0,16},{1,17},{2,18},{3,19},{4,20},{5,21},{6,22},{7,23},{8,24},{9,... | collective-permute-start | bytes 3145736 | tf_op jit(solution)/shard_map/ppermute | solution.py:16
  587.0 41.9 %collective-permute-start.3 = (bf16[1,1024,512]{1,2,0:T(8,128)(2,1)}, bf16[1,1024,512]{1,2,0:T(8,128)(2,1)}, u32[]{:S(2)}, u32[]{:S(2)}) collective-permute-start(bf16[1,1024,512]{1,2,0:T(8,128)(2,1)} %copy.685), channel_id=1, source_target_pairs={{0,16},{1,17},{2,18},{3,19},{4,20},{5,21},{6,22},{7,23},{8,24},{9,... | collective-permute-start | bytes 3145736 | tf_op jit(solution)/shard_map/ppermute | solution.py:16
  725.4 467.0 %copy-start.34 = (bf16[1,1024,512]{2,1,0:T(8,128)(2,1)S(1)}, bf16[1,1024,512]{2,1,0:T(8,128)(2,1)}, u32[]{:S(2)}) copy-start(bf16[1,1024,512]{2,1,0:T(8,128)(2,1)} %get-tuple-element.5722) | copy-start | bytes 3145732
  725.4 467.0 %copy-start.106 = (f32[1,1024,512]{2,1,0:T(8,128)S(1)}, f32[1,1024,512]{2,1,0:T(8,128)}, u32[]{:S(2)}) copy-start(f32[1,1024,512]{2,1,0:T(8,128)} %get-tuple-element.10336) | copy-start | bytes 6291460
  725.4 467.0 %copy-start.276 = (f32[1,512]{1,0:T(1,128)S(1)}, f32[1,512]{1,0:T(1,128)}, u32[]{:S(2)}) copy-start(f32[1,512]{1,0:T(1,128)} %get-tuple-element.5736) | copy-start | bytes 6148
  728.1 443.7 %collective-permute-start.4 = (bf16[1,1024,512]{2,1,0:T(8,128)(2,1)}, bf16[1,1024,512]{2,1,0:T(8,128)(2,1)}, u32[]{:S(2)}, u32[]{:S(2)}) collective-permute-start(bf16[1,1024,512]{2,1,0:T(8,128)(2,1)} %copy.708), channel_id=1, source_target_pairs={{16,0},{17,1},{18,2},{19,3},{20,4},{21,5},{22,6},{23,7},{24,8},{25... | collective-permute-start | bytes 3145736 | tf_op jit(solution)/shard_map/ppermute | solution.py:16
  732.0 460.4 %collective-permute-start.5 = (bf16[1,1024,512]{2,1,0:T(8,128)(2,1)}, bf16[1,1024,512]{2,1,0:T(8,128)(2,1)S(1)}, u32[]{:S(2)}, u32[]{:S(2)}) collective-permute-start(bf16[1,1024,512]{2,1,0:T(8,128)(2,1)} %copy.709), channel_id=1, source_target_pairs={{16,0},{17,1},{18,2},{19,3},{20,4},{21,5},{22,6},{23,7},{24,8},{25... | collective-permute-start | bytes 3145736 | tf_op jit(solution)/shard_map/ppermute | solution.py:16
  1421.3 162.7 %copy-start.37 = (bf16[1,1024,512]{2,1,0:T(8,128)(2,1)S(1)}, bf16[1,1024,512]{2,1,0:T(8,128)(2,1)}, u32[]{:S(2)}) copy-start(bf16[1,1024,512]{2,1,0:T(8,128)(2,1)} %get-tuple-element.5775) | copy-start | bytes 3145732
  1421.3 162.7 %copy-start.82 = (bf16[1,1024,512]{2,1,0:T(8,128)(2,1)S(1)}, bf16[1,1024,512]{2,1,0:T(8,128)(2,1)}, u32[]{:S(2)}) copy-start(bf16[1,1024,512]{2,1,0:T(8,128)(2,1)} %get-tuple-element.5779) | copy-start | bytes 3145732
  1421.3 162.7 %copy-start.280 = (f32[1,512]{1,0:T(1,128)S(1)}, f32[1,512]{1,0:T(1,128)}, u32[]{:S(2)}) copy-start(f32[1,512]{1,0:T(1,128)} %get-tuple-element.5789) | copy-start | bytes 6148
  1424.0 140.0 %collective-permute-start.6 = (bf16[1,1024,512]{2,1,0:T(8,128)(2,1)}, bf16[1,1024,512]{2,1,0:T(8,128)(2,1)S(1)}, u32[]{:S(2)}, u32[]{:S(2)}) collective-permute-start(bf16[1,1024,512]{2,1,0:T(8,128)(2,1)} %copy.728), channel_id=1, source_target_pairs={{16,0},{17,1},{18,2},{19,3},{20,4},{21,5},{22,6},{23,7},{24,8},{25... | collective-permute-start | bytes 3145736 | tf_op jit(solution)/shard_map/ppermute | solution.py:16
  1427.8 156.2 %collective-permute-start.7 = (bf16[1,1024,512]{2,1,0:T(8,128)(2,1)}, bf16[1,1024,512]{2,1,0:T(8,128)(2,1)S(1)}, u32[]{:S(2)}, u32[]{:S(2)}) collective-permute-start(bf16[1,1024,512]{2,1,0:T(8,128)(2,1)} %copy.729), channel_id=1, source_target_pairs={{16,0},{17,1},{18,2},{19,3},{20,4},{21,5},{22,6},{23,7},{24,8},{25... | collective-permute-start | bytes 3145736 | tf_op jit(solution)/shard_map/ppermute | solution.py:16
  1600.6 39.3 %copy-start.256 = (f32[1024]{0:T(1024)}, f32[1024]{0:T(1024)S(1)}, u32[]{:S(2)}) copy-start(f32[1024]{0:T(1024)S(1)} %negate_multiply_fusion.16) | copy-start | bytes 12292 | tf_op jit(solution)/shard_map/transpose(jvp())/cond
  1815.8 118.3 %reduce-scatter.9.cloned.1.call-start = ((), (), s32[]{:S(2)}) async-start(), calls=%async_computation.11 | async-start | bytes 2228224 | tf_op jit(solution)/shard_map/reduce_scatter | solution.py:548
  1820.9 178.6 %reduce-scatter.13.cloned.1.call-start = ((), (), s32[]{:S(2)}) async-start(), calls=%async_computation.13 | async-start | bytes 2228224 | tf_op jit(solution)/shard_map/reduce_scatter | solution.py:544
  1826.0 249.7 %reduce-scatter.11.cloned.1.call-start = ((), (), s32[]{:S(2)}) async-start(), calls=%async_computation.12 | async-start | bytes 4456448 | tf_op jit(solution)/shard_map/reduce_scatter | solution.py:543
  1834.6 317.3 %reduce-scatter.15.cloned.1.call-start = ((), (), s32[]{:S(2)}) async-start(), calls=%async_computation.14 | async-start | bytes 4456448 | tf_op jit(solution)/shard_map/reduce_scatter | solution.py:545
  1843.1 384.8 %reduce-scatter.17.cloned.1.call-start = ((), (), s32[]{:S(2)}) async-start(), calls=%async_computation.15 | async-start | bytes 4456448 | tf_op jit(solution)/shard_map/reduce_scatter | solution.py:546
  (125 other events, 756.2 us)
Sparse Core Ops, SparseCore 0:
  10.7 40.7 all-gather.5
  54.3 36.8 all-gather.9
  93.9 40.3 all-gather.7
  136.9 40.1 all-gather.11
  179.7 40.1 all-gather.13
  1815.9 53.1 reduce-scatter.18
  1873.4 60.6 reduce-scatter.8
  1938.9 60.5 reduce-scatter.12
  2003.9 71.6 reduce-scatter.10
  2080.4 71.4 reduce-scatter.14
  2156.3 71.5 reduce-scatter.16
where the time goes:
time: 2250 us; the launch traced here: 2230 us
  waiting for transfers between devices  1220 us (54%)
  matrix products  343 us (15%)
  local copies, waits for them, and re-layouts  335 us (15%)
  other arithmetic  172 us (8%)
  loops' own time  88.2 us (4%)
  starting transfers between devices  40.1 us (2%)
  blocking collectives  23.8 us (1%)
    ppermute x8, waiting for transfers between devices, from_behind(): return lax.ppermute(shard, axis, pairs)  682 us
    another operation x97, local copies, waits for them, and re-layouts  130 us
    dot_general x28, matrix products, encode_section(): attention(queries, key_rows, value_rows, segment_rows, segment_rows, quer...  130 us
    reduce_scatter x1, waiting for transfers between devices, body(): lax.psum_scatter(summed[2], 'dp', scatter_dimension=0, tiled=True)  76.2 us
    reduce_scatter x1, waiting for transfers between devices, body(): lax.psum_scatter(summed[0], 'dp', scatter_dimension=1, tiled=True)  76.2 us
    reduce_scatter x1, waiting for transfers between devices, body(): lax.psum_scatter(summed[3], 'dp', scatter_dimension=0, tiled=True)  76 us
    dot_general x6, matrix products, feed(): product(normed, up_weight)  73.7 us
    another operation x6, loops' own time, run_section(): lax.switch(branch, [spare_section, encode_section, decode_section], weigh...  73.6 us
  transfers between devices with their start and end apart: 19, of which 19 were waited for; matrix products, arithmetic and copies ran while one was open for 4% of the time, Pallas kernels for 0%

commit v1 on v0

v1 whole, which is shorter than its diff:
```python
from functools import partial

import jax
import jax.numpy as jnp
from jax import lax
from jax.experimental import pallas as pl
from jax.experimental.pallas import tpu as pltpu
from jax.sharding import PartitionSpec as P

BF = jnp.bfloat16
F32 = jnp.float32
DH = 64
PAIR = 2 * DH
QB = 128
WIN = 256
TB = 256
VMEM_BYTES = 60 * 1024 * 1024


def nn(left, right):
    return jnp.dot(left, right, preferred_element_type=F32)


def nt(left, right):
    return lax.dot_general(left, right, (((1,), (1,)), ((), ())), preferred_element_type=F32)


def tn(left, right):
    return lax.dot_general(left, right, (((0,), (0,)), ((), ())), preferred_element_type=F32)


def norm_parts(stream):
    centred = stream - jnp.mean(stream, axis=-1, keepdims=True)
    scale = lax.rsqrt(jnp.mean(centred * centred, axis=-1, keepdims=True) + 1e-05)
    return centred * scale, scale


def norm_back(grad, unit, scale, gain):
    inner = grad * gain
    first = jnp.mean(inner, axis=-1, keepdims=True)
    second = jnp.mean(inner * unit, axis=-1, keepdims=True)
    return scale * (inner - first - unit * second), jnp.sum(grad * unit, axis=0, keepdims=True)


def block_at(index, size):
    return pl.ds(pl.multiple_of(index * size, size), size)


def lane_halves(scale=1.0):
    lane = lax.broadcasted_iota(jnp.int32, (1, PAIR), 1)
    low = jnp.where(lane < DH, scale, 0.0).astype(BF)
    high = jnp.where(lane < DH, 0.0, scale).astype(BF)
    return low, high


def both_heads(block, halves):
    return jnp.concatenate([block * halves[0], block * halves[1]], axis=0)


def join_heads(stacked):
    lane = lax.broadcasted_iota(jnp.int32, (QB, PAIR), 1)
    return jnp.where(lane < DH, stacked[:QB], stacked[QB:])


def window_start(index, length):
    return pl.multiple_of(jnp.clip(index * QB - DH, 0, length - WIN), DH)


def mask_bias(index, start, cols_ref, rows_ref, causal):
    keys = cols_ref[pl.ds(start, WIN), :]
    query_segment = rows_ref[0, pl.ds(index, 1), :]
    if causal:
        query_level = rows_ref[1, pl.ds(index, 1), :]
        key_id = start + lax.broadcasted_iota(jnp.int32, (WIN, QB), 0)
        query_id = index * QB + lax.broadcasted_iota(jnp.int32, (WIN, QB), 1)
        allowed = (keys[:, 1:2] == query_segment) & (
            (keys[:, 2:3] < query_level) | (key_id == query_id)
        )
    else:
        allowed = keys[:, 0:1] == query_segment
    bias = jnp.where(allowed, 0.0, -1e30)
    return jnp.concatenate([bias, bias], axis=1)


def attend_block(index, q_ref, k_ref, v_ref, cols_ref, rows_ref, weights_ref, mixed_ref, causal):
    length, width = q_ref.shape
    start = window_start(index, length)
    rows = block_at(index, QB)
    bias = mask_bias(index, start, cols_ref, rows_ref, causal)
    halves = lane_halves(DH ** -0.5)
    for pair in range(width // PAIR):
        lanes = slice(pair * PAIR, (pair + 1) * PAIR)
        queries = both_heads(q_ref[rows, lanes], halves)
        scores = nt(k_ref[pl.ds(start, WIN), lanes], queries) + bias
        shifted = jnp.exp(scores - jnp.max(scores, axis=0, keepdims=True))
        weights = (shifted * (1.0 / jnp.sum(shifted, axis=0, keepdims=True))).astype(BF)
        weights_ref[index, pair] = weights
        out = tn(weights, v_ref[pl.ds(start, WIN), lanes])
        mixed_ref[rows, lanes] = join_heads(out).astype(BF)


def attend_back_block(
    index, q_ref, k_ref, v_ref, weights_ref, mixed_ref, dmixed_ref, dq_ref, dk_ref, dv_ref
):
    length, width = q_ref.shape
    start = window_start(index, length)
    rows = block_at(index, QB)
    window = pl.ds(start, WIN)
    plain = lane_halves()
    halves = lane_halves(DH ** -0.5)
    ones = jnp.ones((WIN, PAIR), BF)
    for pair in range(width // PAIR):
        lanes = slice(pair * PAIR, (pair + 1) * PAIR)
        queries = both_heads(q_ref[rows, lanes], halves)
        keys = k_ref[window, lanes]
        values = v_ref[window, lanes]
        weights = weights_ref[index, pair]
        dmixed = dmixed_ref[rows, lanes]
        grads = both_heads(dmixed, plain)
        inner = (dmixed.astype(F32) * mixed_ref[rows, lanes].astype(F32) * -1.0).astype(BF)
        left = jnp.concatenate([values, ones], axis=1)
        right = jnp.concatenate([grads, both_heads(inner, plain)], axis=1)
        centred = nt(left, right)
        dscores = (weights.astype(F32) * centred).astype(BF)
        dv_ref[window, lanes] += nn(weights, grads)
        dk_ref[window, lanes] += nn(dscores, queries)
        dq = tn(dscores, keys) * (DH ** -0.5)
        dq_ref[rows, lanes] = join_heads(dq).astype(BF)


def gelu_parts(value):
    cdf = 0.5 + 0.5 * lax.erf(value * (0.5 ** 0.5))
    density = jnp.exp(value * value * -0.5) * 0.3989422804014327
    return value * cdf, cdf + value * density


def feed_block(normed, up_ref, down_ref, hidden_ref, slope_ref, rows):
    total = None
    width = up_ref.shape[1]
    step = 512
    for at in range(0, width, step):
        hidden, slope = gelu_parts(nn(normed, up_ref[:, at : at + step]))
        hidden = hidden.astype(BF)
        hidden_ref[rows, at : at + step] = hidden
        slope_ref[rows, at : at + step] = slope.astype(BF)
        term = nn(hidden, down_ref[at : at + step, :])
        total = term if total is None else total + term
    return total


def feed_back_block(grad, up_ref, down_ref, slope_ref, rows):
    total = None
    width = up_ref.shape[1]
    step = 512
    for at in range(0, width, step):
        dhidden = nt(grad, down_ref[at : at + step, :])
        dup = (dhidden * slope_ref[rows, at : at + step].astype(F32)).astype(BF)
        slope_ref[rows, at : at + step] = dup
        term = nt(dup, up_ref[:, at : at + step])
        total = term if total is None else total + term
    return total


def loop(count, body):
    def step(index, carry):
        body(index)
        return carry

    lax.fori_loop(0, count, step, 0)


def put_grad(out_ref, index, value, prior_ref):
    if prior_ref is not None:
        value = value + prior_ref[index].astype(F32)
    out_ref[index] = value.astype(BF)


def weight_grad(out_ref, prior_ref, left_t_ref, right_ref, transposed):
    step = 512
    width = right_ref.shape[1]

    def slab(index):
        cols = block_at(index, step)
        value = nn(left_t_ref[...], right_ref[:, cols])
        if transposed:
            put_grad(out_ref, (cols, slice(None)), value.T, prior_ref)
        else:
            put_grad(out_ref, (slice(None), cols), value, prior_ref)

    loop(width // step, slab)


def encode_kernel(
    src, table, gains, mats, up, down, cols, rows_in, mem, qkv, weights, mixed, x1, x2, hidden, slope
):
    length = src.shape[0]

    def project(index):
        rows = block_at(index, TB)
        unit, _ = norm_parts(src[rows, :].astype(F32) + table[rows, :].astype(F32))
        normed = (unit * gains[0:1, :]).astype(BF)
        for which in range(3):
            qkv[which, rows, :] = nn(normed, mats[which]).astype(BF)

    loop(length // TB, project)

    def rest(index):
        for part in range(TB // QB):
            attend_block(
                index * (TB // QB) + part,
                qkv.at[0], qkv.at[1], qkv.at[2], cols, rows_in, weights, mixed, False,
            )
        rows = block_at(index, TB)
        stream = src[rows, :].astype(F32) + table[rows, :].astype(F32)
        stream = stream + nn(mixed[rows, :], mats[3])
        x1[rows, :] = stream
        unit, _ = norm_parts(stream)
        normed = (unit * gains[1:2, :]).astype(BF)
        stream = stream + feed_block(normed, up, down, hidden, slope, rows)
        x2[rows, :] = stream
        unit, _ = norm_parts(stream)
        mem[rows, :] = (unit * gains[2:3, :]).astype(BF)

    loop(length // TB, rest)


def encode_back_kernel(prior, *refs):
    (src, table, gains, mats, up, down, qkv, weights, mixed, x1, x2, hidden, slope_in, dmem) = refs[:14]
    refs = refs[14:]
    if prior:
        p_mats, p_up, p_down, p_table, p_gains = refs[:5]
        refs = refs[5:]
    else:
        p_mats = p_up = p_down = p_table = p_gains = None
    (g_in, g_mats, g_up, g_down, g_table, g_gains) = refs[:6]
    (slope, dy, dy_t, a_t, dx, dmixed, dq, dk, dv) = refs[6:]
    length = src.shape[0]
    slope[...] = slope_in[...]
    g_gains[...] = jnp.zeros_like(g_gains) if p_gains is None else p_gains[...]
    dk[...] = jnp.zeros_like(dk)
    dv[...] = jnp.zeros_like(dv)

    def feed_step(index):
        rows = block_at(index, TB)
        unit, scale = norm_parts(x2[rows, :])
        grad, d_gain = norm_back(dmem[rows, :].astype(F32), unit, scale, gains[2:3, :])
        g_gains[2:3, :] += d_gain
        low = grad.astype(BF)
        dy_t[:, rows] = low.T
        dnormed = feed_back_block(low, up, down, slope, rows)
        unit, scale = norm_parts(x1[rows, :])
        a_t[:, rows] = (unit * gains[1:2, :]).astype(BF).T
        back, d_gain = norm_back(dnormed, unit, scale, gains[1:2, :])
        g_gains[1:2, :] += d_gain
        grad = grad + back
        dx[rows, :] = grad
        low = grad.astype(BF)
        dy[rows, :] = low
        dmixed[rows, :] = nt(low, mats[3]).astype(BF)

    loop(length // TB, feed_step)
    weight_grad(g_up, p_up, a_t, slope, False)
    weight_grad(g_down, p_down, dy_t, hidden, True)
    put_grad(g_mats, 3, tn(mixed[...], dy[...]), p_mats)

    def attend_step(index):
        attend_back_block(
            index, qkv.at[0], qkv.at[1], qkv.at[2], weights, mixed, dmixed, dq, dk, dv
        )

    loop(length // QB, attend_step)

    def project_step(index):
        rows = block_at(index, TB)
        unit, scale = norm_parts(src[rows, :].astype(F32) + table[rows, :].astype(F32))
        a_t[:, rows] = (unit * gains[0:1, :]).astype(BF).T
        dnormed = nt(dq[rows, :], mats[0])
        dnormed += nt(dk[rows, :].astype(BF), mats[1])
        dnormed += nt(dv[rows, :].astype(BF), mats[2])
        back, d_gain = norm_back(dnormed, unit, scale, gains[0:1, :])
        g_gains[0:1, :] += d_gain
        grad = dx[rows, :] + back
        g_in[rows, :] = grad
        put_grad(g_table, (slice(None), rows), grad.T, p_table)

    loop(length // TB, project_step)
    put_grad(g_mats, 0, nn(a_t[...], dq[...]), p_mats)
    put_grad(g_mats, 1, nn(a_t[...], dk[...].astype(BF)), p_mats)
    put_grad(g_mats, 2, nn(a_t[...], dv[...].astype(BF)), p_mats)


def self_kernel(tgt, table, gains, mats, cols, rows_in, qkv, weights, mixed, h1):
    length = tgt.shape[0]

    def project(index):
        rows = block_at(index, TB)
        stream = table[rows, :].astype(F32)
        unit, _ = norm_parts(stream)
        qkv[0, rows, :] = nn((unit * gains[0:1, :]).astype(BF), mats[0]).astype(BF)
        unit, _ = norm_parts(tgt[rows, :].astype(F32) + stream)
        normed = (unit * gains[0:1, :]).astype(BF)
        for which in (1, 2):
            qkv[which, rows, :] = nn(normed, mats[which]).astype(BF)

    loop(length // TB, project)

    def rest(index):
        for part in range(TB // QB):
            attend_block(
                index * (TB // QB) + part,
                qkv.at[0], qkv.at[1], qkv.at[2], cols, rows_in, weights, mixed, True,
            )
        rows = block_at(index, TB)
        h1[rows, :] = table[rows, :].astype(F32) + nn(mixed[rows, :], mats[3])

    loop(length // TB, rest)


def self_back_kernel(prior, *refs):
    (tgt, table, gains, mats, qkv, weights, mixed, dh1) = refs[:8]
    refs = refs[8:]
    if prior:
        p_mats, p_table, p_gains = refs[:3]
        refs = refs[3:]
    else:
        p_mats = p_table = p_gains = None
    (g_in, g_mats, g_table, g_gains) = refs[:4]
    (dy, a_t, b_t, dmixed, dq, dk, dv) = refs[4:]
    length = tgt.shape[0]
    g_gains[...] = jnp.zeros_like(g_gains) if p_gains is None else p_gains[...]
    dk[...] = jnp.zeros_like(dk)
    dv[...] = jnp.zeros_like(dv)

    def out_step(index):
        rows = block_at(index, TB)
        low = dh1[rows, :].astype(BF)
        dy[rows, :] = low
        dmixed[rows, :] = nt(low, mats[3]).astype(BF)

    loop(length // TB, out_step)
    put_grad(g_mats, 3, tn(mixed[...], dy[...]), p_mats)

    def attend_step(index):
        attend_back_block(
            index, qkv.at[0], qkv.at[1], qkv.at[2], weights, mixed, dmixed, dq, dk, dv
        )

    loop(length // QB, attend_step)

    def project_step(index):
        rows = block_at(index, TB)
        stream = table[rows, :].astype(F32)
        unit, scale = norm_parts(stream)
        a_t[:, rows] = (unit * gains[0:1, :]).astype(BF).T
        back, d_gain = norm_back(nt(dq[rows, :], mats[0]), unit, scale, gains[0:1, :])
        dtable = dh1[rows, :] + back
        unit, scale = norm_parts(tgt[rows, :].astype(F32) + stream)
        b_t[:, rows] = (unit * gains[0:1, :]).astype(BF).T
        dnormed = nt(dk[rows, :].astype(BF), mats[1])
        dnormed += nt(dv[rows, :].astype(BF), mats[2])
        back, d_gain_too = norm_back(dnormed, unit, scale, gains[0:1, :])
        g_gains[0:1, :] += d_gain + d_gain_too
        g_in[rows, :] = back
        put_grad(g_table, (slice(None), rows), (dtable + back).T, p_table)

    loop(length // TB, project_step)
    put_grad(g_mats, 0, nn(a_t[...], dq[...]), p_mats)
    put_grad(g_mats, 1, nn(b_t[...], dk[...].astype(BF)), p_mats)
    put_grad(g_mats, 2, nn(b_t[...], dv[...].astype(BF)), p_mats)


def cross_kernel(prior, *refs):
    (h1, mem, cot, gains, mats, up, down, cols, rows_in) = refs[:9]
    refs = refs[9:]
    if prior:
        p_mats, p_up, p_down, p_gains = refs[:4]
        refs = refs[4:]
    else:
        p_mats = p_up = p_down = p_gains = None
    (out, dmem, dh1, g_mats, g_up, g_down, g_gains) = refs[:7]
    (qkv, weights, mixed, h2, hidden, slope, dy, dy_t, a_t, dmixed, dq, dk, dv) = refs[7:]
    length = h1.shape[0]
    g_gains[...] = jnp.zeros_like(g_gains) if p_gains is None else p_gains[...]
    dk[...] = jnp.zeros_like(dk)
    dv[...] = jnp.zeros_like(dv)

    def project(index):
        rows = block_at(index, TB)
        unit, _ = norm_parts(h1[rows, :])
        qkv[0, rows, :] = nn((unit * gains[1:2, :]).astype(BF), mats[0]).astype(BF)
        qkv[1, rows, :] = nn(mem[rows, :], mats[2]).astype(BF)
        qkv[2, rows, :] = nn(mem[rows, :], mats[3]).astype(BF)

    loop(length // TB, project)

    def middle(index):
        for part in range(TB // QB):
            attend_block(
                index * (TB // QB) + part,
                qkv.at[0], qkv.at[1], qkv.at[2], cols, rows_in, weights, mixed, False,
            )
        rows = block_at(index, TB)
        stream = h1[rows, :] + nn(mixed[rows, :], mats[1])
        h2[rows, :] = stream
        unit, scale = norm_parts(stream)
        normed = (unit * gains[2:3, :]).astype(BF)
        a_t[:, rows] = normed.T
        out[rows, :] = (stream + feed_block(normed, up, down, hidden, slope, rows)).astype(BF)
        low = cot[rows, :]
        dy_t[:, rows] = low.T
        dnormed = feed_back_block(low, up, down, slope, rows)
        back, d_gain = norm_back(dnormed, unit, scale, gains[2:3, :])
        g_gains[2:3, :] += d_gain
        grad = low.astype(F32) + back
        h2[rows, :] = grad
        low = grad.astype(BF)
        dy[rows, :] = low
        dmixed[rows, :] = nt(low, mats[1]).astype(BF)

    loop(length // TB, middle)

    def attend_step(index):
        attend_back_block(
            index, qkv.at[0], qkv.at[1], qkv.at[2], weights, mixed, dmixed, dq, dk, dv
        )

    loop(length // QB, attend_step)

    weight_grad(g_up, p_up, a_t, slope, False)
    weight_grad(g_down, p_down, dy_t, hidden, True)
    put_grad(g_mats, 1, tn(mixed[...], dy[...]), p_mats)

    def project_step(index):
        rows = block_at(index, TB)
        unit, scale = norm_parts(h1[rows, :])
        a_t[:, rows] = (unit * gains[1:2, :]).astype(BF).T
        back, d_gain = norm_back(nt(dq[rows, :], mats[0]), unit, scale, gains[1:2, :])
        g_gains[1:2, :] += d_gain
        dh1[rows, :] = h2[rows, :] + back
        dkeys = dk[rows, :].astype(BF)
        dvalues = dv[rows, :].astype(BF)
        dmem[rows, :] = (nt(dkeys, mats[2]) + nt(dvalues, mats[3])).astype(BF)

    loop(length // TB, project_step)
    put_grad(g_mats, 0, nn(a_t[...], dq[...]), p_mats)
    put_grad(g_mats, 2, tn(mem[...], dk[...].astype(BF)), p_mats)
    put_grad(g_mats, 3, tn(mem[...], dv[...].astype(BF)), p_mats)


def shape(dims, kind):
    return jax.ShapeDtypeStruct(dims, kind)


def call(kernel, name, outs, scratch, *args):
    return pl.pallas_call(
        kernel,
        out_shape=outs,
        in_specs=[pl.BlockSpec(memory_space=pltpu.VMEM)] * len(args),
        out_specs=[pl.BlockSpec(memory_space=pltpu.VMEM)] * len(outs),
        scratch_shapes=[pltpu.VMEM(s.shape, s.dtype) for s in scratch],
        compiler_params=pltpu.CompilerParams(vmem_limit_bytes=VMEM_BYTES),
        name=name,
    )(*args)


def sizes(length, width, ff):
    blocks = length // QB
    pairs = width // PAIR
    return dict(
        tok=shape((length, width), BF),
        tok32=shape((length, width), F32),
        qkv=shape((3, length, width), BF),
        weights=shape((blocks, pairs, WIN, 2 * QB), BF),
        hidden=shape((length, ff), BF),
        tokt=shape((width, length), BF),
        mats=shape((4, width, width), BF),
        up=shape((width, ff), BF),
        down=shape((ff, width), BF),
        gains=shape((8, width), F32),
    )


def encode(z, src, table, gains, mats, up, down, cols, rows):
    outs = [z["tok"], z["qkv"], z["weights"], z["tok"], z["tok32"], z["tok32"], z["hidden"], z["hidden"]]
    return call(encode_kernel, "encode", outs, [], src, table, gains, mats, up, down, cols, rows)


def encode_back(z, src, table, gains, mats, up, down, kept, dmem, prior):
    outs = [z["tok32"], z["mats"], z["up"], z["down"], z["tokt"], z["gains"]]
    scratch = [z["hidden"], z["tok"], z["tokt"], z["tokt"], z["tok32"], z["tok"], z["tok"], z["tok32"], z["tok32"]]
    return call(
        partial(encode_back_kernel, len(prior) > 0), "encode_back", outs, scratch,
        src, table, gains, mats, up, down, *kept, dmem, *prior,
    )


def self_forward(z, tgt, table, gains, mats, cols, rows):
    outs = [z["qkv"], z["weights"], z["tok"], z["tok32"]]
    return call(self_kernel, "self_forward", outs, [], tgt, table, gains, mats, cols, rows)


def self_back(z, tgt, table, gains, mats, kept, dh1, prior):
    outs = [z["tok32"], z["mats"], z["tokt"], z["gains"]]
    scratch = [z["tok"], z["tokt"], z["tokt"], z["tok"], z["tok"], z["tok32"], z["tok32"]]
    return call(
        partial(self_back_kernel, len(prior) > 0), "self_back", outs, scratch,
        tgt, table, gains, mats, *kept, dh1, *prior,
    )


def cross(z, h1, mem, cot, gains, mats, up, down, cols, rows, prior):
    outs = [z["tok"], z["tok"], z["tok32"], z["mats"], z["up"], z["down"], z["gains"]]
    scratch = [
        z["qkv"], z["weights"], z["tok"], z["tok32"], z["hidden"], z["hidden"], z["tok"], z["tokt"],
        z["tokt"], z["tok"], z["tok"], z["tok32"], z["tok32"],
    ]
    return call(
        partial(cross_kernel, len(prior) > 0), "cross", outs, scratch,
        h1, mem, cot, gains, mats, up, down, cols, rows, *prior,
    )


def unset(outs):
    return pl.pallas_call(
        lambda *refs: None,
        out_shape=outs,
        out_specs=[pl.BlockSpec(memory_space=pl.ANY)] * len(outs),
        name="unset",
    )()


def to_section(value, source):
    return lax.ppermute(value, "section", [(source, 1 - source)])


def gather(value, axis):
    return lax.all_gather(value, "dp", axis=axis, tiled=True)


def scatter(value, axis):
    return lax.psum_scatter(value, "dp", scatter_dimension=axis, tiled=True)


def mask_arrays(segments, levels):
    first = jnp.concatenate(
        [jnp.ones_like(segments[:, :1], bool), segments[:, 1:] != segments[:, :-1]], axis=1
    )
    usable = jnp.where((levels[0] > 0) | first, segments, -1)
    cols = jnp.stack([usable, segments, levels[1]] + [segments] * 5, axis=-1)
    rows = jnp.stack([segments, levels[1]], axis=1)
    return cols, rows.reshape(rows.shape[0], 2, -1, QB)


def body(
    inputs,
    positions,
    projections,
    out_projections,
    ffn_up,
    ffn_down,
    norm_gains,
    segments,
    levels,
    cotangent,
):
    encoder = lax.axis_index("section") == 0
    own = inputs[0, :, 0]
    cot = cotangent[:, 0]
    micro, length, width = own.shape
    z = sizes(length, width, ffn_up.shape[2])
    cols, rows = mask_arrays(segments[:, 0], levels[:, :, 0])

    proj, outp = projections[0].astype(BF), out_projections[0].astype(BF)
    lent = to_section(jnp.stack([proj[3], outp[1]]), 0)
    own_mats = jnp.stack([proj[0], proj[1], proj[2], outp[0]])
    cross_mats = jnp.concatenate([jnp.stack([proj[3], outp[1]]), lent])
    mats = gather(own_mats, 1)
    mats_b = gather(cross_mats, 1)
    up = gather(ffn_up[0].astype(BF), 0)
    down = gather(ffn_down[0].astype(BF), 0)
    table = gather(positions[0].astype(BF), 1)
    gains = gather(norm_gains[0].astype(BF), 1).astype(F32)
    gains = jnp.concatenate([gains, jnp.zeros((5, width), F32)])

    attn = [z["qkv"], z["weights"], z["tok"], z["tok32"]]
    extra = [z["tok32"], z["hidden"], z["hidden"]]

    def first_encoder(m):
        mem, *kept = encode(z, own[m], table, gains, mats, up, down, cols[m], rows[m])
        return (mem, *kept)

    def first_decoder(m):
        kept = self_forward(z, own[m], table, gains, mats, cols[m], rows[m])
        return (*unset([z["tok"]]), *kept, *unset(extra))

    kept, mems, sent = [], [], []
    for m in range(micro):
        mem, *rest = lax.cond(encoder, partial(first_encoder, m), partial(first_decoder, m))
        kept.append(rest)
        sent.append(mem)
        mems.append(to_section(mem, 0))

    crossed = [z["tok"], z["tok"], z["tok32"], z["mats"], z["up"], z["down"], z["gains"]]
    outs, dmems, dh1s, prior = [], [], [], ()
    for m in range(micro):

        def middle_decoder():
            return tuple(
                cross(z, kept[m][3], mems[m], cot[m], gains, mats_b, up, down, cols[m], rows[m], prior)
            )

        def middle_encoder():
            return tuple(unset(crossed))

        out, dmem, dh1, *prior = lax.cond(encoder, middle_encoder, middle_decoder)
        outs.append(out)
        dmems.append(to_section(dmem, 1))
        dh1s.append(dh1)
    g_cross, g_up, g_down, g_gains = prior

    g_ins, prior = [], ()
    for m in reversed(range(micro)):
        def last_encoder():
            g_in, *grads = encode_back(
                z, own[m], table, gains, mats, up, down, kept[m], dmems[m], prior
            )
            return (g_in, *grads)

        def last_decoder():
            less = (prior[0], prior[3], prior[4]) if prior else ()
            g_in, g_mats, g_table, g_gains = self_back(
                z, own[m], table, gains, mats, kept[m][:3], dh1s[m], less
            )
            return (g_in, g_mats, *unset([z["up"], z["down"]]), g_table, g_gains)

        g_in, *prior = lax.cond(encoder, last_encoder, last_decoder)
        g_ins.insert(0, g_in)
    s_mats, s_up, s_down, s_table, s_gains = prior
    s_up = jnp.where(encoder, s_up, g_up)
    s_down = jnp.where(encoder, s_down, g_down)
    s_gains = s_gains + jnp.where(encoder, 0.0, g_gains)

    r_mats = scatter(s_mats, 1)
    r_cross = scatter(g_cross, 1)
    r_up = scatter(s_up, 0)
    r_down = scatter(s_down, 0)
    r_table = scatter(s_table, 0).T
    r_gains = scatter(s_gains, 1)[:3]
    back = to_section(r_cross[2:], 1)
    own_cross = jnp.where(encoder, back, r_cross[:2])
    d_proj = jnp.concatenate([r_mats[:3], own_cross[:1]]).astype(F32)
    d_out = jnp.concatenate([r_mats[3:], own_cross[1:]]).astype(F32)

    main = [jnp.where(encoder, kept_mem, out) for kept_mem, out in zip(sent, outs)]
    return (
        jnp.stack(main)[None, :, None],
        jnp.stack(g_ins)[None, :, None],
        r_table.astype(F32)[None],
        d_proj[None],
        d_out[None],
        r_up.astype(F32)[None],
        r_down.astype(F32)[None],
        r_gains[None],
    )


def solution(mesh):
    in_specs = (
        P("section", None, "dp", None, None),
        P("section", None, "dp"),
        P("section", None, "dp", None),
        P("section", None, "dp", None),
        P("section", "dp", None),
        P("section", "dp", None),
        P("section", None, "dp"),
        P(None, "dp", None),
        P(None, None, "dp", None),
        P(None, "dp", None, None),
    )
    out_specs = (
        P("section", None, "dp", None, None),
        P("section", None, "dp", None, None),
        P("section", None, "dp"),
        P("section", None, "dp", None),
        P("section", None, "dp", None),
        P("section", "dp", None),
        P("section", "dp", None),
        P("section", None, "dp"),
    )
    return jax.shard_map(body, mesh=mesh, in_specs=in_specs, out_specs=out_specs, check_vma=False)
```

time: 2250 us -> 864 us (0.38)
  waiting for transfers between devices: 1220 us -> 607 us
  matrix products: 343 us -> 0 us
  local copies, waits for them, and re-layouts: 335 us -> 31.7 us
  other arithmetic: 172 us -> 24.9 us
  Pallas kernels: 0 us -> 139 us
  loops' own time: 88.2 us -> 1.01 us
  starting transfers between devices: 40.1 us -> 13.9 us
    ppermute x8 -> x6, waiting for transfers between devices: 682 us -> 126 us  [to_section(): return lax.ppermute(value, 'section', [(source, 1 - source)])]
    dot_general x76 -> x0, matrix products: 343 us -> none  [the longest x28 130 us: encode_section(): attention(queries, key_rows, value_rows, segment_rows, segment_rows, quer...]
    pallas_call x0 -> x6, Pallas kernels: none -> 139 us  [the longest x4 139 us: call(): pl.pallas_call(kernel, out_shape=outs, in_specs=[pl.BlockSpec(memory_spac...]
    another operation x97 -> x7, local copies, waits for them, and re-layouts: 130 us -> 8.87 us
    another operation x10 -> x6, loops' own time: 88.2 us -> 1.01 us  [the longest x2 0.4 us: body(): g_in, *prior = lax.cond(encoder, last_encoder, last_decoder)]
    cond x163 -> x6, local copies, waits for them, and re-layouts: 67.2 us -> 0.01 us  [the longest x14 41.1 us: run_section(): lax.switch(branch, [spare_section, encode_section, decode_section], weigh...]
    reduce_scatter x5, waiting for transfers between devices: 357 us -> 308 us  [scatter(): return lax.psum_scatter(value, 'dp', scatter_dimension=axis, tiled=True)]
    dynamic_update_slice x20 -> x0, local copies, waits for them, and re-layouts: 45.9 us -> none  [encode_section(): attention(queries, key_rows, value_rows, segment_rows, segment_rows, quer...]
  transfers between devices with their start and end apart: 19 -> 17, of which waited for: 19 -> 13; matrix products, arithmetic and copies ran while one was open for 4% -> 5% of each run, Pallas kernels for 0% -> 11%
where the time goes in v1:
time: 864 us; the launch traced here: 855 us
  waiting for transfers between devices  607 us (70%)
  Pallas kernels  139 us (16%)
  local copies, waits for them, and re-layouts  31.7 us (4%)
  other arithmetic  24.9 us (3%)
  blocking collectives  22.4 us (3%)
  between operations  14.5 us (2%)
  starting transfers between devices  13.9 us (2%)
    reduce_scatter x5, waiting for transfers between devices, scatter(): return lax.psum_scatter(value, 'dp', scatter_dimension=axis, tiled=True)  308 us
    pallas_call x4, Pallas kernels, call(): pl.pallas_call(kernel, out_shape=outs, in_specs=[pl.BlockSpec(memory_spac...  139 us
    all_gather x5, waiting for transfers between devices, gather(): return lax.all_gather(value, 'dp', axis=axis, tiled=True)  136 us
    ppermute x6, waiting for transfers between devices, to_section(): return lax.ppermute(value, 'section', [(source, 1 - source)])  126 us
    unnamed x12, waiting for transfers between devices  37.9 us
    all_gather x1, blocking collectives, gather(): return lax.all_gather(value, 'dp', axis=axis, tiled=True)  22.4 us
  transfers between devices with their start and end apart: 17, of which 13 were waited for; matrix products, arithmetic and copies ran while one was open for 5% of the time, Pallas kernels for 11%

profile of v1, /device:TPU:0, one launch (start us, length us, event | category | flops | bytes accessed | tf_op | source)
XLA Modules:
  0.0 854.7 jit_solution(15546699213302371122)
XLA Ops:
  14.1 4.9 collective-permute-start.1
  21.8 22.4 %all-gather.1 = bf16[1,3,512]{1,0,2:T(2,128)(2,1)S(1)} all-gather(bf16[1,3,32]{1,0,2:T(2,128)(2,1)S(1)} %copy.76), channel_id=3, replica_groups=mesh['section'=2,'dp'=16] {'dp'}, dimensions={2}, use_global_device_ids=true | all-gather | bytes 3264 | tf_op jit(solution)/shard_map/all_gather | solution.py:537
  44.6 6.9 all-gather.14.cloned.1.call-done
  51.5 43.2 %all-gather.10.cloned.1.call-done = bf16[4,512,512]{2,1,0:T(8,128)(2,1)} async-done(((bf16[4,32,512]{2,1,0:T(8,128)(2,1)}), bf16[4,512,512]{2,1,0:T(8,128)(2,1)}) %all-gather.10.cloned.1.call-update) | async-done | bytes 2097168 | tf_op jit(solution)/shard_map/all_gather | solution.py:537
  94.7 43.0 %all-gather.16.cloned.1.call-done = bf16[1,512,2048]{2,1,0:T(8,128)(2,1)} async-done(((bf16[1,32,2048]{2,1,0:T(8,128)(2,1)}), bf16[1,512,2048]{2,1,0:T(8,128)(2,1)}) %all-gather.16.cloned.1.call-update) | async-done | bytes 2097168 | tf_op jit(solution)/shard_map/all_gather | solution.py:537
  137.6 42.8 %all-gather.18.cloned.1.call-done = bf16[1,2048,512]{2,1,0:T(8,128)(2,1)} async-done(((bf16[1,128,512]{2,1,0:T(8,128)(2,1)}), bf16[1,2048,512]{2,1,0:T(8,128)(2,1)}) %all-gather.18.cloned.1.call-update) | async-done | bytes 2097168 | tf_op jit(solution)/shard_map/all_gather | solution.py:537
  180.4 34.1 %conditional.6 = ((bf16[1024,512]{1,0:T(8,128)(2,1)S(1)}, bf16[3,1024,512]{2,1,0:T(8,128)(2,1)}, bf16[8,4,256,256]{3,2,1,0:T(8,128)(2,1)}, bf16[1024,512]{1,0:T(...) conditional(s32[]{:T(128)} %convert_element_type.67, ...), branch_computations={%region_0.1_spmd, %region_1.2_spmd} | conditional | bytes 12796004 | solution.py:598
  181.0 2.3 copy.81.table
  184.5 2.3 slice_bitcast_fusion.3.src
  186.7 27.7 %encode.2 = (bf16[1024,512]{1,0:T(8,128)(2,1)S(1)}, bf16[3,1024,512]{2,1,0:T(8,128)(2,1)}, bf16[8,4,256,256]{3,2,1,0:T(8,128)(2,1)}, bf16[1024,512]{1,0:T(8,128)...) custom-call(bf16[1024,512]{1,0:T(8,128)(2,1)} %slice_bitcast_fusion., ...), custom_call_target="tpu_custom_call" | custom-call | tf_op jit(solution)/shard_map/cond/branch_1_fun/encode/pallas_call | solution.py:455
  214.5 2.3 collective-permute-start
  216.8 35.4 %conditional.8 = ((bf16[1024,512]{1,0:T(8,128)(2,1)}, bf16[3,1024,512]{2,1,0:T(8,128)(2,1)}, bf16[8,4,256,256]{3,2,1,0:T(8,128)(2,1)}, bf16[1024,512]{1,0:T(8,12...) conditional(s32[]{:T(128)} %convert_element_type.67, ...), branch_computations={%region_4.5_spmd, %region_5.6_spmd} | conditional | bytes 12796004 | solution.py:598
  217.6 2.3 copy.86.table
  223.1 2.3 slice_bitcast_fusion.12.src
  225.3 26.9 %encode.3 = (bf16[1024,512]{1,0:T(8,128)(2,1)}, bf16[3,1024,512]{2,1,0:T(8,128)(2,1)}, bf16[8,4,256,256]{3,2,1,0:T(8,128)(2,1)}, bf16[1024,512]{1,0:T(8,128)(2,1...) custom-call(bf16[1024,512]{1,0:T(8,128)(2,1)} %slice_bitcast_fusion.12.s, ...), custom_call_target="tpu_custom_call" | custom-call | tf_op jit(solution)/shard_map/cond/branch_1_fun/encode/pallas_call | solution.py:455
  254.5 22.4 %collective-permute-done.2 = bf16[1024,512]{1,0:T(8,128)(2,1)} collective-permute-done((bf16[1024,512]{1,0:T(8,128)(2,1)}, bf16[1024,512]{1,0:T(8,128)(2,1)}, u32[]{:S(2)}, u32[]{:S(2)}) %collective-permute-start.2) | collective-permute-done | bytes 1048608 | tf_op jit(solution)/shard_map/ppermute | solution.py:533
  280.1 101.5 %collective-permute-done.3 = bf16[1024,512]{1,0:T(8,128)(2,1)} collective-permute-done((bf16[1024,512]{1,0:T(8,128)(2,1)}, bf16[1024,512]{1,0:T(8,128)(2,1)}, u32[]{:S(2)}, u32[]{:S(2)}) %collective-permute-start.3) | collective-permute-done | bytes 1048608 | tf_op jit(solution)/shard_map/ppermute | solution.py:533
  381.6 44.8 %conditional.10 = ((f32[1024,512]{1,0:T(8,128)}, bf16[4,512,512]{2,1,0:T(8,128)(2,1)}, bf16[512,2048]{1,0:T(8,128)(2,1)}, bf16[2048,512]{1,0:T(8,128)(2,1)}, bf1...) conditional(s32[]{:T(128)} %convert_element_type.67, (bf16[2,1024,512]{2,1,0:T(8,128)(2,1)}, ...), branch_computations={%region_8.9_spmd, %region_9.10_spmd} | conditional | bytes 4194360 | solution.py:636
  383.1 2.3 slice_bitcast_fusion.19.refs_0_
  385.4 41.0 %encode_back.2 = (f32[1024,512]{1,0:T(8,128)}, bf16[4,512,512]{2,1,0:T(8,128)(2,1)}, bf16[512,2048]{1,0:T(8,128)(2,1)}, bf16[2048,512]{1,0:T(8,128)(2,1)}, bf16[...) custom-call(bf16[1024,512]{1,0:T(8,128)(2,1)} %slice_bitcast_fusion.19.refs_0_, bf16[1024,512]{1,0:T(8,128)(2,1)} %copy.89.refs_1_, ...), custom_call_target="tpu_custom_call" | custom-call | tf_op jit(solution)/shard_map/cond/branch_1_fun/encode_back/pallas_call | solution.py:455
  426.4 47.5 %conditional.11 = ((f32[1024,512]{1,0:T(8,128)}, bf16[4,512,512]{2,1,0:T(8,128)(2,1)}, bf16[512,2048]{1,0:T(8,128)(2,1)}, bf16[2048,512]{1,0:T(8,128)(2,1)}, bf1...) conditional(s32[]{:T(128)} %convert_element_type.67, (bf16[2,1024,512]{2,1,0:T(8,128)(2,1)}, ...), branch_computations={%region_10.11_spmd, %region_11.12_spmd} | conditional | bytes 8388692 | solution.py:636
  428.0 2.4 slice_bitcast_fusion.21.refs_0_
  430.3 43.6 %encode_back.3 = (f32[1024,512]{1,0:T(8,128)}, bf16[4,512,512]{2,1,0:T(8,128)(2,1)}, bf16[512,2048]{1,0:T(8,128)(2,1)}, bf16[2048,512]{1,0:T(8,128)(2,1)}, bf16[...) custom-call(bf16[1024,512]{1,0:T(8,128)(2,1)} %slice_bitcast_fusion.21.refs_0_, bf16[1024,512]{1,0:T(8,128)(2,1)} %copy.91.refs_1_, ...), custom_call_target="tpu_custom_call" | custom-call | tf_op jit(solution)/shard_map/cond/branch_1_fun/encode_back/pallas_call | solution.py:455
  477.1 3.1 broadcast_select_fusion
  481.9 3.3 broadcast_select_fusion.1
  489.9 2.5 maximum_bitcast_fusion
  492.4 35.7 %reduce-scatter.19.cloned.1.call-done = f32[32,8]{1,0:T(8,128)} async-done(((f32[512,8]{1,0:T(8,128)}), f32[32,8]{1,0:T(8,128)}) %reduce-scatter.19.cloned.1.call-update) | async-done | bytes 1040
  529.4 63.0 %reduce-scatter.13.cloned.1.call-done = bf16[4,32,512]{2,1,0:T(8,128)(2,1)} async-done(((bf16[4,512,512]{2,1,0:T(8,128)(2,1)}), bf16[4,32,512]{2,1,0:T(8,128)(2,1)}) %reduce-scatter.13.cloned.1.call-update) | async-done | bytes 131088 | tf_op jit(solution)/shard_map/reduce_scatter | solution.py:541
  594.5 58.4 %reduce-scatter.9.cloned.1.call-done = bf16[32,1024]{1,0:T(8,128)(2,1)} async-done(((bf16[512,1024]{1,0:T(8,128)(2,1)}), bf16[32,1024]{1,0:T(8,128)(2,1)}) %reduce-scatter.9.cloned.1.call-update) | async-done | bytes 65552 | tf_op jit(solution)/shard_map/reduce_scatter | solution.py:541
  655.3 61.9 %reduce-scatter.11.cloned.1.call-done = bf16[4,32,512]{2,1,0:T(8,128)(2,1)} async-done(((bf16[4,512,512]{2,1,0:T(8,128)(2,1)}), bf16[4,32,512]{2,1,0:T(8,128)(2,1)}) %reduce-scatter.11.cloned.1.call-update) | async-done | bytes 131088 | tf_op jit(solution)/shard_map/reduce_scatter | solution.py:541
  720.3 61.6 %reduce-scatter.17.cloned.1.call-done = bf16[128,512]{1,0:T(8,128)(2,1)} async-done(((bf16[2048,512]{1,0:T(8,128)(2,1)}), bf16[128,512]{1,0:T(8,128)(2,1)}) %reduce-scatter.17.cloned.1.call-update) | async-done | bytes 131088 | tf_op jit(solution)/shard_map/reduce_scatter | solution.py:541
  783.5 62.7 %reduce-scatter.15.cloned.1.call-done = bf16[32,2048]{1,0:T(8,128)(2,1)} async-done(((bf16[512,2048]{1,0:T(8,128)(2,1)}), bf16[32,2048]{1,0:T(8,128)(2,1)}) %reduce-scatter.15.cloned.1.call-update) | async-done | bytes 131088 | tf_op jit(solution)/shard_map/reduce_scatter | solution.py:541
  (121 shorter events, 45.1 us)
Async XLA Ops:
  7.2 6.1 copy-start.18
  7.2 14.4 %copy-start.20 = (f32[1,3,32]{2,0,1:T(1,128)S(1)}, f32[1,3,32]{2,0,1:T(1,128)}, u32[]{:S(2)}) copy-start(f32[1,3,32]{2,0,1:T(1,128)} %param.28) | copy-start | bytes 1156
  7.2 14.4 %copy-start.19 = (s32[2,2,1,1024]{3,2,1,0:T(1,128)S(1)}, s32[2,2,1,1024]{3,2,1,0:T(1,128)}, u32[]{:S(2)}) copy-start(s32[2,2,1,1024]{3,2,1,0:T(1,128)} %param.30) | copy-start | bytes 49156
  7.2 14.4 %copy-start.17 = (s32[2,1,1024]{2,1,0:T(1,128)S(1)}, s32[2,1,1024]{2,1,0:T(1,128)}, u32[]{:S(2)}) copy-start(s32[2,1,1024]{2,1,0:T(1,128)} %param.29) | copy-start | bytes 24580
  7.2 44.3 %all-gather.14.cloned.1.call-start = ((), (), s32[]{:S(2)}) async-start(), calls=%async_computation.13 | async-start | bytes 1114112 | tf_op jit(solution)/shard_map/all_gather | solution.py:537
  8.9 85.8 %all-gather.10.cloned.1.call-start = ((), (), s32[]{:S(2)}) async-start(), calls=%async_computation.6 | async-start | bytes 2228224 | tf_op jit(solution)/shard_map/all_gather | solution.py:537
  11.5 126.1 %all-gather.16.cloned.1.call-start = ((), (), s32[]{:S(2)}) async-start(), calls=%async_computation.14 | async-start | bytes 2228224 | tf_op jit(solution)/shard_map/all_gather | solution.py:537
  13.2 167.2 %all-gather.18.cloned.1.call-start = ((), (), s32[]{:S(2)}) async-start(), calls=%async_computation.15 | async-start | bytes 2228224 | tf_op jit(solution)/shard_map/all_gather | solution.py:537
  14.0 240.5 %all-gather.12.cloned.1.call-start = ((), (), s32[]{:S(2)}) async-start(), calls=%async_computation.7 | async-start | bytes 2228224 | tf_op jit(solution)/shard_map/all_gather | solution.py:537
  14.1 6.8 collective-permute-start.1
  21.5 506.5 %reduce-scatter.19.cloned.1.call-start = ((), (), s32[]{:S(2)}) async-start(), calls=%async_computation.16 | async-start | bytes 278528
  183.3 3.4 copy-start.2
  214.5 2.3 copy-start.9
  214.5 40.0 %collective-permute-start = (bf16[1024,512]{1,0:T(8,128)(2,1)S(1)}, bf16[1024,512]{1,0:T(8,128)(2,1)}, u32[]{:S(2)}, u32[]{:S(2)}) collective-permute-start(bf16[1024,512]{1,0:T(8,128)(2,1)S(1)} %get-tuple-element.382), channel_id=1, source_target_pairs={{0,16},{1,17},{2,18},{3,19},{4,20},{5,21},{6,22},{7,23},{8,24},{9,... | collective-permute-start | bytes 3145736 | tf_op jit(solution)/shard_map/ppermute | solution.py:533
  219.9 5.5 copy-start.4
  252.2 24.7 %collective-permute-start.2 = (bf16[1024,512]{1,0:T(8,128)(2,1)}, bf16[1024,512]{1,0:T(8,128)(2,1)}, u32[]{:S(2)}, u32[]{:S(2)}) collective-permute-start(bf16[1024,512]{1,0:T(8,128)(2,1)} %get-tuple-element.385), channel_id=1, source_target_pairs={{0,16},{1,17},{2,18},{3,19},{4,20},{5,21},{6,22},{7,23},{8,24},{9,... | collective-permute-start | bytes 3145736 | tf_op jit(solution)/shard_map/ppermute | solution.py:533
  276.9 104.7 %copy-start = (bf16[4,512,512]{2,1,0:T(8,128)(2,1)S(1)}, bf16[4,512,512]{2,1,0:T(8,128)(2,1)}, u32[]{:S(2)}) copy-start(bf16[4,512,512]{2,1,0:T(8,128)(2,1)} %all-gather.10.cloned.1.call-done) | copy-start | bytes 6291460
  276.9 104.7 %copy-start.6 = (bf16[1,1024,512]{1,2,0:T(8,128)(2,1)S(1)}, bf16[1,1024,512]{1,2,0:T(8,128)(2,1)}, u32[]{:S(2)}) copy-start(bf16[1,1024,512]{1,2,0:T(8,128)(2,1)} %all-gather.14.cloned.1.call-done) | copy-start | bytes 3145732
  277.3 104.3 %collective-permute-start.3 = (bf16[1024,512]{1,0:T(8,128)(2,1)}, bf16[1024,512]{1,0:T(8,128)(2,1)}, u32[]{:S(2)}, u32[]{:S(2)}) collective-permute-start(bf16[1024,512]{1,0:T(8,128)(2,1)} %get-tuple-element.403), channel_id=1, source_target_pairs={{16,0},{17,1},{18,2},{19,3},{20,4},{21,5},{22,6},{23,7},{24,8},{25... | collective-permute-start | bytes 3145736 | tf_op jit(solution)/shard_map/ppermute | solution.py:533
  278.8 147.6 %collective-permute-start.4 = (bf16[1024,512]{1,0:T(8,128)(2,1)}, bf16[1024,512]{1,0:T(8,128)(2,1)}, u32[]{:S(2)}, u32[]{:S(2)}) collective-permute-start(bf16[1024,512]{1,0:T(8,128)(2,1)} %get-tuple-element.410), channel_id=1, source_target_pairs={{16,0},{17,1},{18,2},{19,3},{20,4},{21,5},{22,6},{23,7},{24,8},{25... | collective-permute-start | bytes 3145736 | tf_op jit(solution)/shard_map/ppermute | solution.py:533
  427.9 2.4 copy-start.8
  474.8 117.6 %reduce-scatter.13.cloned.1.call-start = ((), (), s32[]{:S(2)}) async-start(), calls=%async_computation.10 | async-start | bytes 2228224 | tf_op jit(solution)/shard_map/reduce_scatter | solution.py:541
  475.5 1.6 copy-start.13
  475.6 177.4 %reduce-scatter.9.cloned.1.call-start = ((), (), s32[]{:S(2)}) async-start(), calls=%async_computation.8 | async-start | bytes 1114112 | tf_op jit(solution)/shard_map/reduce_scatter | solution.py:541
  476.3 240.9 %reduce-scatter.11.cloned.1.call-start = ((), (), s32[]{:S(2)}) async-start(), calls=%async_computation.9 | async-start | bytes 2228224 | tf_op jit(solution)/shard_map/reduce_scatter | solution.py:541
  477.0 304.8 %reduce-scatter.17.cloned.1.call-start = ((), (), s32[]{:S(2)}) async-start(), calls=%async_computation.12 | async-start | bytes 2228224 | tf_op jit(solution)/shard_map/reduce_scatter | solution.py:541
  480.3 1.6 copy-start.12
  480.3 365.9 %reduce-scatter.15.cloned.1.call-start = ((), (), s32[]{:S(2)}) async-start(), calls=%async_computation.11 | async-start | bytes 2228224 | tf_op jit(solution)/shard_map/reduce_scatter | solution.py:541
  481.9 3.3 copy-start.16
  486.9 2.4 copy-start.14
  486.9 3.0 copy-start.15
  593.2 61.2 %collective-permute-start.5 = (bf16[2,32,512]{2,1,0:T(8,128)(2,1)S(1)}, bf16[2,32,512]{2,1,0:T(8,128)(2,1)S(1)}, u32[]{:S(2)}, u32[]{:S(2)}) collective-permute-start(bf16[2,32,512]{2,1,0:T(8,128)(2,1)S(1)} %slice.163), channel_id=1, source_target_pairs={{16,0},{17,1},{18,2},{19,3},{20,4},{21,5},{22,6},{23,7},{24,8},{25... | collective-permute-start | bytes 196616 | tf_op jit(solution)/shard_map/ppermute | solution.py:533
  (2 other events, 2.8 us)
Sparse Core Ops, SparseCore 0:
  10.8 40.6 all-gather.13
  54.2 40.3 all-gather.9
  97.4 40.1 all-gather.15
  140.2 40.1 all-gather.17
  183.0 40.1 all-gather.11
  474.9 53.0 reduce-scatter.18
  531.8 60.5 reduce-scatter.12
  596.4 56.4 reduce-scatter.8
  656.7 60.4 reduce-scatter.10
  721.3 60.5 reduce-scatter.16
  785.6 60.5 reduce-scatter.14

commit v2 on v1

--- a/solution.py
+++ b/solution.py
@@ -520,6 +520,393 @@
     )
 
 
+LINE = 4
+TABLE_ROWS = 48
+MESH = pl.DeviceIdType.MESH
+
+
+def place():
+    me = lax.axis_index("dp")
+    return me // 4, (me // 2) % 2, me % 2
+
+
+def rank_of(z, x, core):
+    return z * 4 + x * 2 + core
+
+
+def at_rank(ref, axis, per, rank):
+    rows = pl.ds(pl.multiple_of(rank * per, per), per)
+    return ref.at[rows, :] if axis == 0 else ref.at[:, rows, :]
+
+
+def greet(z, x, core):
+    barrier = pltpu.get_barrier_semaphore()
+
+    def signal(rank):
+        pl.semaphore_signal(barrier, inc=1, device_id={"dp": rank}, device_id_type=MESH)
+
+    signal(rank_of(z, 1 - x, core))
+    signal(rank_of(z, x, 1 - core))
+
+    for step in range(1, LINE):
+        signal(rank_of((z + step) % LINE, x, core))
+    pl.semaphore_wait(barrier, LINE + 1)
+
+
+def remote(src, dst, send, recv, rank):
+    return pltpu.make_async_remote_copy(
+        src_ref=src, dst_ref=dst, send_sem=send, recv_sem=recv, device_id={"dp": rank},
+        device_id_type=MESH,
+    )
+
+
+def gather_kernel(
+    proj, outp, up, down, pos, gain, o_mats, o_up, o_down, o_table, s_mats, s_up, s_down, s_table,
+    zsend, zrecv, xsend, xrecv, csend, crecv, here,
+):
+    z, x, core = place()
+    for to, (ref, index) in enumerate(
+        ((proj, 0), (proj, 1), (proj, 2), (outp, 0), (proj, 3), (outp, 1))
+    ):
+        s_mats[to] = ref[index].astype(BF)
+    s_up[...] = up[...].astype(BF)
+    s_down[...] = down[...].astype(BF)
+    per = pos.shape[1]
+    s_table[...] = jnp.zeros_like(s_table)
+    s_table[:per, :] = pos[...].T.astype(BF)
+    s_table[per : per + gain.shape[0], :per] = gain[...].astype(BF)
+    greet(z, x, core)
+
+    outs = ((o_mats, 1), (o_up, 0), (o_down, 0), (o_table, 0))
+    mine = (s_mats, s_up, s_down, s_table)
+    pers = (s_mats.shape[1], s_up.shape[0], s_down.shape[0], s_table.shape[0])
+    kinds = range(len(outs))
+
+    def view(kind, rank):
+        return at_rank(outs[kind][0], outs[kind][1], pers[kind], rank)
+
+    across = rank_of(z, 1 - x, core)
+    sibling = rank_of(z, x, 1 - core)
+    own = rank_of(z, x, core)
+
+    def along(kind, way, step, src, rank):
+        return remote(
+            src, view(kind, rank), zsend.at[kind, way, step], zrecv.at[kind, way, step],
+            rank_of(z + (1 - 2 * way), x, core),
+        )
+
+    def over(kind, slot, src, rank):
+        return remote(src, view(kind, rank), xsend.at[kind, slot], xrecv.at[kind, slot], across)
+
+    def beside(kind, slot, src, rank):
+        return remote(src, view(kind, rank), csend.at[kind, slot], crecv.at[kind, slot], sibling)
+
+    def can_send(way):
+        return (z > 0) if way else (z < LINE - 1)
+
+    slots = [(0, 0, 0)] + [(1 + way * 3 + step, way, step + 1) for step in range(3) for way in range(2)]
+
+    def begins(way, back):
+        return z - back * (1 - 2 * way)
+
+    def exists(way, back):
+        if back == 0:
+            return None
+        return (z <= LINE - 1 - back) if way else (z >= back)
+
+    def when(cond, do):
+        if cond is None:
+            do()
+        else:
+            pl.when(cond)(do)
+
+    local = [pltpu.make_async_copy(mine[k], view(k, own), here.at[k]) for k in kinds]
+    for kind in kinds:
+        for way in range(2):
+
+            @pl.when(can_send(way))
+            def _():
+                along(kind, way, 0, mine[kind], own).start()
+
+        over(kind, 0, mine[kind], own).start()
+    for kind in kinds:
+        beside(kind, 0, mine[kind], own).start()
+        local[kind].start()
+
+    for slot, way, back in slots[1:]:
+
+        def pass_on():
+            rank = rank_of(begins(way, back), x, core)
+            for kind in kinds:
+                block = view(kind, rank)
+                along(kind, way, back - 1, block, rank).wait_recv()
+                if back < LINE - 1:
+
+                    @pl.when(can_send(way))
+                    def _():
+                        along(kind, way, back, block, rank).start()
+
+                over(kind, slot, block, rank).start()
+                beside(kind, slot, block, rank).start()
+
+        when(exists(way, back), pass_on)
+
+    for slot, way, back in slots:
+
+        def share():
+            rank = rank_of(begins(way, back), 1 - x, core)
+            for kind in kinds:
+                block = view(kind, rank)
+                over(kind, slot, block, rank).wait_recv()
+                beside(kind, 7 + slot, block, rank).start()
+
+        when(exists(way, back), share)
+
+    for kind in kinds:
+        local[kind].wait()
+        for way in range(2):
+            for step in range(3):
+                sent = can_send(way)
+                if step > 0:
+                    sent = sent & exists(way, step)
+
+                @pl.when(sent)
+                def _():
+                    along(kind, way, step, mine[kind], own).wait_send()
+
+    for slot, way, back in slots:
+
+        def finish():
+            for kind in kinds:
+                over(kind, slot, mine[kind], own).wait_send()
+                for part in range(2):
+                    copy = beside(kind, slot + 7 * part, mine[kind], own)
+                    copy.wait_send()
+                    copy.wait_recv()
+
+        when(exists(way, back), finish)
+
+
+def gather_weights(proj, outp, up, down, pos, gain):
+    ranks = lax.axis_size("dp")
+    count, per, width = proj.shape[0] + outp.shape[0], proj.shape[1], proj.shape[2]
+    length = pos.shape[0]
+    if ranks != 4 * LINE or per != pos.shape[1] or per + gain.shape[0] > TABLE_ROWS:
+        order = [proj[0], proj[1], proj[2], outp[0], proj[3], outp[1]]
+        every = lambda value, axis: lax.all_gather(value.astype(BF), "dp", axis=axis, tiled=True)
+        return (
+            every(jnp.stack(order), 1), every(up, 0), every(down, 0),
+            every(pos, 1), every(gain, 1),
+        )
+    shards = [
+        shape((count, per, width), BF), shape(up.shape, BF), shape(down.shape, BF),
+        shape((TABLE_ROWS, length), BF),
+    ]
+    outs = [
+        shape((count, per * ranks, width), BF), shape((up.shape[0] * ranks, up.shape[1]), BF),
+        shape((down.shape[0] * ranks, width), BF), shape((TABLE_ROWS * ranks, length), BF),
+    ]
+    dma = pltpu.SemaphoreType.DMA
+    mats, up, down, packed = pl.pallas_call(
+        gather_kernel,
+        out_shape=outs,
+        in_specs=[pl.BlockSpec(memory_space=pltpu.VMEM)] * 6,
+        out_specs=[pl.BlockSpec(memory_space=pl.ANY)] * 4,
+        scratch_shapes=[pltpu.VMEM(s.shape, s.dtype) for s in shards]
+        + [dma((4, 2, 3)), dma((4, 2, 3)), dma((4, 7)), dma((4, 7)), dma((4, 14)), dma((4, 14)), dma((4,))],
+        compiler_params=pltpu.CompilerParams(
+            collective_id=0, has_side_effects=True, vmem_limit_bytes=VMEM_BYTES
+        ),
+        name="gather",
+    )(proj, outp, up, down, pos, gain)
+    packed = packed.reshape(ranks, TABLE_ROWS, length)
+    table = packed[:, :per].reshape(ranks * per, length).T
+    gains = packed[:, per : per + gain.shape[0], :per].transpose(1, 0, 2).reshape(-1, width)
+    return mats, up, down, table, gains
+
+
+def scatter_kernel(
+    g_mats, g_up, g_down, g_table, g_gain, o_mats, o_up, o_down, o_table, o_gain,
+    c_mats, c_up, c_down, c_table, x_mats, x_up, x_down, x_table, z_mats, z_up, z_down, z_table,
+    gain_buf, csend, crecv, xsend, xrecv, zsend, zrecv, gsend, grecv,
+):
+    z, x, core = place()
+    greet(z, x, core)
+    across = rank_of(z, 1 - x, core)
+    sibling = rank_of(z, x, 1 - core)
+    own = rank_of(z, x, core)
+    grads = ((g_mats, 1), (g_up, 0), (g_down, 0), (g_table, 0))
+    outs = (o_mats, o_up, o_down, o_table)
+    cbuf = (c_mats, c_up, c_down, c_table)
+    xbuf = (x_mats, x_up, x_down, x_table)
+    zbuf = (z_mats, z_up, z_down, z_table)
+    kinds = range(4)
+    order = (3, 0, 2, 1)
+
+    def grad(kind, rank):
+        ref, axis = grads[kind]
+        return at_rank(ref, axis, outs[kind].shape[axis], rank)
+
+    def beside(kind, dest, part):
+        target_x = x if part else 1 - x
+        return remote(
+            grad(kind, rank_of(dest, target_x, 1 - core)), cbuf[kind].at[dest, part],
+            csend.at[kind, dest, part], crecv.at[kind, dest, part], sibling,
+        )
+
+    def over(kind, dest):
+        return remote(
+            cbuf[kind].at[dest, 0], xbuf[kind].at[dest], xsend.at[kind, dest], xrecv.at[kind, dest], across
+        )
+
+    def along(kind, dest, way):
+        return remote(
+            cbuf[kind].at[dest, 1], zbuf[kind].at[dest, way], zsend.at[kind, dest, way],
+            zrecv.at[kind, dest, way], rank_of(z + (1 - 2 * way), x, core),
+        )
+
+    def add(into, *others):
+        total = into[...].astype(F32)
+        for other in others:
+            total = total + other[...].astype(F32)
+        into[...] = total.astype(BF)
+
+    for kind in kinds:
+        for dest in order:
+            for part in range(2):
+                beside(kind, dest, part).start()
+    for kind in kinds:
+        for dest in order:
+            beside(kind, dest, 0).wait_recv()
+            add(cbuf[kind].at[dest, 0], grad(kind, rank_of(dest, 1 - x, core)))
+            over(kind, dest).start()
+
+    for kind in kinds:
+        for dest in order:
+            beside(kind, dest, 1).wait_recv()
+            over(kind, dest).wait_recv()
+            add(cbuf[kind].at[dest, 1], grad(kind, rank_of(dest, x, core)), xbuf[kind].at[dest])
+            for way in range(2):
+                before = (z > dest) if way else (z < dest)
+                far = (z == LINE - 1) if way else (z == 0)
+
+                @pl.when(before)
+                def _():
+                    @pl.when(jnp.logical_not(far))
+                    def _():
+                        along(kind, dest, way).wait_recv()
+                        add(cbuf[kind].at[dest, 1], zbuf[kind].at[dest, way])
+
+                    along(kind, dest, way).start()
+
+    for kind in kinds:
+        for dest in range(LINE):
+
+            @pl.when(z == dest)
+            def _():
+                total = cbuf[kind][dest, 1].astype(F32)
+                if dest > 0:
+                    along(kind, dest, 0).wait_recv()
+                    total = total + zbuf[kind][dest, 0].astype(F32)
+                if dest < LINE - 1:
+                    along(kind, dest, 1).wait_recv()
+                    total = total + zbuf[kind][dest, 1].astype(F32)
+                outs[kind][...] = total
+
+    for kind in kinds:
+        for dest in order:
+            over(kind, dest).wait_send()
+            for part in range(2):
+                beside(kind, dest, part).wait_send()
+            for way in range(2):
+
+                @pl.when((z > dest) if way else (z < dest))
+                def _():
+                    along(kind, dest, way).wait_send()
+
+    gain_buf[0] = g_gain[...]
+
+    def swap(index, rank):
+        return remote(gain_buf.at[0], gain_buf.at[index], gsend.at[index], grecv.at[index], rank)
+
+    for index, rank in ((1, sibling), (2, across)):
+        copy = swap(index, rank)
+        copy.start()
+        copy.wait_send()
+        copy.wait_recv()
+        gain_buf[0] = gain_buf[0] + gain_buf[index]
+    for way in range(2):
+        for step in range(1, LINE):
+            ahead = z + step * (1 - 2 * way)
+            there = (z >= step) if way else (z <= LINE - 1 - step)
+
+            @pl.when(there)
+            def _():
+                swap(2 + way * 3 + step, rank_of(ahead, x, core)).start()
+
+    for way in range(2):
+        for step in range(1, LINE):
+            behind = (z <= LINE - 1 - step) if way else (z >= step)
+
+            @pl.when(behind)
+            def _():
+                swap(2 + way * 3 + step, own).wait_recv()
+
+    for way in range(2):
+        for step in range(1, LINE):
+            there = (z >= step) if way else (z <= LINE - 1 - step)
+
+            @pl.when(there)
+            def _():
+                swap(2 + way * 3 + step, own).wait_send()
+
+    o_gain[...] = gain_buf[0]
+    for way in range(2):
+        for step in range(1, LINE):
+            behind = (z <= LINE - 1 - step) if way else (z >= step)
+
+            @pl.when(behind)
+            def _():
+                o_gain[...] = o_gain[...] + gain_buf[2 + way * 3 + step]
+
+
+def scatter_grads(mats, up, down, table, gains):
+    ranks = lax.axis_size("dp")
+    count, width = mats.shape[0], mats.shape[1]
+    per = width // ranks
+    if ranks != 4 * LINE:
+        part = lambda value, axis: lax.psum_scatter(
+            value, "dp", scatter_dimension=axis, tiled=True
+        ).astype(F32)
+        return part(mats, 1), part(up, 0), part(down, 0), part(table, 0).T, part(gains, 1)[:3]
+    shards = [
+        (count, per, width), (up.shape[0] // ranks, up.shape[1]), (down.shape[0] // ranks, width),
+        (table.shape[0] // ranks, table.shape[1]),
+    ]
+    dma = pltpu.SemaphoreType.DMA
+    outs = pl.pallas_call(
+        scatter_kernel,
+        out_shape=[shape(s, F32) for s in shards] + [shape(gains.shape, F32)],
+        in_specs=[pl.BlockSpec(memory_space=pltpu.VMEM)] * 5,
+        out_specs=[pl.BlockSpec(memory_space=pltpu.VMEM)] * 5,
+        scratch_shapes=[pltpu.VMEM((LINE, 2) + s, BF) for s in shards]
+        + [pltpu.VMEM((LINE,) + s, BF) for s in shards]
+        + [pltpu.VMEM((LINE, 2) + s, BF) for s in shards]
+        + [pltpu.VMEM((9,) + gains.shape, F32)]
+        + [
+            dma((4, LINE, 2)), dma((4, LINE, 2)), dma((4, LINE)), dma((4, LINE)), dma((4, LINE, 2)),
+            dma((4, LINE, 2)), dma((9,)), dma((9,)),
+        ],
+        compiler_params=pltpu.CompilerParams(
+            collective_id=1, has_side_effects=True, vmem_limit_bytes=VMEM_BYTES
+        ),
+        name="scatter",
+    )(mats, up, down, table, gains)
+    mats, up, down, table, gains = outs
+    gains = lax.dynamic_slice_in_dim(gains, lax.axis_index("dp") * per, per, 1)[:3]
+    return mats, up, down, table.T, gains
+
+
 def unset(outs):
     return pl.pallas_call(
         lambda *refs: None,
@@ -531,14 +918,6 @@
 
 def to_section(value, source):
     return lax.ppermute(value, "section", [(source, 1 - source)])
-
-
-def gather(value, axis):
-    return lax.all_gather(value, "dp", axis=axis, tiled=True)
-
-
-def scatter(value, axis):
-    return lax.psum_scatter(value, "dp", scatter_dimension=axis, tiled=True)
 
 
 def mask_arrays(segments, levels):
@@ -570,17 +949,12 @@
     z = sizes(length, width, ffn_up.shape[2])
     cols, rows = mask_arrays(segments[:, 0], levels[:, :, 0])
 
-    proj, outp = projections[0].astype(BF), out_projections[0].astype(BF)
-    lent = to_section(jnp.stack([proj[3], outp[1]]), 0)
-    own_mats = jnp.stack([proj[0], proj[1], proj[2], outp[0]])
-    cross_mats = jnp.concatenate([jnp.stack([proj[3], outp[1]]), lent])
-    mats = gather(own_mats, 1)
-    mats_b = gather(cross_mats, 1)
-    up = gather(ffn_up[0].astype(BF), 0)
-    down = gather(ffn_down[0].astype(BF), 0)
-    table = gather(positions[0].astype(BF), 1)
-    gains = gather(norm_gains[0].astype(BF), 1).astype(F32)
-    gains = jnp.concatenate([gains, jnp.zeros((5, width), F32)])
+    mats_all, up, down, table, gains = gather_weights(
+        projections[0], out_projections[0], ffn_up[0], ffn_down[0], positions[0], norm_gains[0]
+    )
+    mats, lent = mats_all[:4], to_section(mats_all[4:], 0)
+    mats_b = jnp.concatenate([mats_all[4:], lent])
+    gains = jnp.concatenate([gains.astype(F32), jnp.zeros((5, width), F32)])
 
     attn = [z["qkv"], z["weights"], z["tok"], z["tok32"]]
     extra = [z["tok32"], z["hidden"], z["hidden"]]
@@ -640,26 +1014,21 @@
     s_down = jnp.where(encoder, s_down, g_down)
     s_gains = s_gains + jnp.where(encoder, 0.0, g_gains)
 
-    r_mats = scatter(s_mats, 1)
-    r_cross = scatter(g_cross, 1)
-    r_up = scatter(s_up, 0)
-    r_down = scatter(s_down, 0)
-    r_table = scatter(s_table, 0).T
-    r_gains = scatter(s_gains, 1)[:3]
-    back = to_section(r_cross[2:], 1)
-    own_cross = jnp.where(encoder, back, r_cross[:2])
-    d_proj = jnp.concatenate([r_mats[:3], own_cross[:1]]).astype(F32)
-    d_out = jnp.concatenate([r_mats[3:], own_cross[1:]]).astype(F32)
+    returned = to_section(g_cross[2:], 1)
+    s_mats = jnp.concatenate([s_mats, jnp.where(encoder, returned, g_cross[:2])])
+    r_mats, r_up, r_down, r_table, r_gains = scatter_grads(s_mats, s_up, s_down, s_table, s_gains)
+    d_proj = jnp.stack([r_mats[0], r_mats[1], r_mats[2], r_mats[4]])
+    d_out = jnp.stack([r_mats[3], r_mats[5]])
 
     main = [jnp.where(encoder, kept_mem, out) for kept_mem, out in zip(sent, outs)]
     return (
         jnp.stack(main)[None, :, None],
         jnp.stack(g_ins)[None, :, None],
-        r_table.astype(F32)[None],
+        r_table[None],
         d_proj[None],
         d_out[None],
-        r_up.astype(F32)[None],
-        r_down.astype(F32)[None],
+        r_up[None],
+        r_down[None],
         r_gains[None],
     )
 

time: 864 us -> 475 us (0.55)
  waiting for transfers between devices: 607 us -> 119 us
  Pallas kernels: 139 us -> 273 us
  blocking collectives: 22.4 us -> 0 us
  between operations: 14.5 us -> 1.07 us
    reduce_scatter x5 -> x0, waiting for transfers between devices: 308 us -> none  [scatter(): return lax.psum_scatter(value, 'dp', scatter_dimension=axis, tiled=True)]
    all_gather x5 -> x0, waiting for transfers between devices: 136 us -> none  [gather(): return lax.all_gather(value, 'dp', axis=axis, tiled=True)]
    pallas_call x0 -> x2, Pallas kernels: none -> 135 us  [the longest x1 74.9 us: scatter_grads(): pl.pallas_call(scatter_kernel, out_shape=[shape(s, F32) for s in shards]...]
    unnamed x12 -> x0, waiting for transfers between devices: 37.9 us -> none
    all_gather x1 -> x0, blocking collectives: 22.4 us -> none  [gather(): return lax.all_gather(value, 'dp', axis=axis, tiled=True)]
  transfers between devices with their start and end apart: 17 -> 6, of which waited for: 13 -> 2; matrix products, arithmetic and copies ran while one was open for 5% -> 8% of each run, Pallas kernels for 11% -> 30%
where the time goes in v2:
time: 475 us; the launch traced here: 467 us
  Pallas kernels  273 us (57%)
  waiting for transfers between devices  119 us (25%)
  local copies, waits for them, and re-layouts  37.8 us (8%)
  other arithmetic  21.2 us (4%)
  starting transfers between devices  12.8 us (3%)
    pallas_call x4, Pallas kernels, call(): pl.pallas_call(kernel, out_shape=outs, in_specs=[pl.BlockSpec(memory_spac...  139 us
    ppermute x6, waiting for transfers between devices, to_section(): return lax.ppermute(value, 'section', [(source, 1 - source)])  119 us
    pallas_call x1, Pallas kernels, scatter_grads(): pl.pallas_call(scatter_kernel, out_shape=[shape(s, F32) for s in shards]...  74.9 us
    pallas_call x1, Pallas kernels, gather_weights(): pl.pallas_call(gather_kernel, out_shape=outs, in_specs=[pl.BlockSpec(memo...  59.6 us
    ppermute x6, starting transfers between devices, to_section(): return lax.ppermute(value, 'section', [(source, 1 - source)])  12.8 us
  transfers between devices with their start and end apart: 6, of which 2 were waited for; matrix products, arithmetic and copies ran while one was open for 8% of the time, Pallas kernels for 30%

profile of v2, /device:TPU:0, one launch (start us, length us, event | category | flops | bytes accessed | tf_op | source)
XLA Modules:
  0.0 467.0 jit_solution(9887849384841682147)
XLA Ops:
  1.9 1.9 copy.40
  3.8 59.6 %gather.1 = (bf16[6,512,512]{2,1,0:T(8,128)(2,1)}, bf16[512,2048]{1,0:T(8,128)(2,1)}, bf16[2048,512]{1,0:T(8,128)(2,1)}, bf16[768,1024]{1,0:T(8,128)(2,1)}) custom-call(f32[4,32,512]{2,1,0:T(8,128)} %bitcast.134, f32[2,32,512]{2,1,0:T(8,128)} %bitcast.138, f32[32,2048]{1,0:T(8,128)} %bitcast.135, f32[128,512]{1,0:T(8,128)} %bitcast.136, ...), custom_call_target="tpu_custom_call" | custom-call | tf_op jit(solution)/shard_map/gather/pallas_call | solution.py:710
  63.4 2.4 slice.125
  65.8 4.4 collective-permute-start.1
  70.8 1.7 slice.124
  72.5 34.4 %conditional.6 = ((bf16[1024,512]{1,0:T(8,128)(2,1)}, bf16[3,1024,512]{2,1,0:T(8,128)(2,1)}, bf16[8,4,256,256]{3,2,1,0:T(8,128)(2,1)}, bf16[1024,512]{1,0:T(8,12...) conditional(s32[]{:T(128)} %convert_element_type.15, ...), branch_computations={%region_0.1_spmd, %region_1.2_spmd} | conditional | bytes 4407368 | solution.py:972
  75.8 1.9 slice_bitcast_fusion.4.cols
  77.7 2.3 slice_bitcast_fusion.3.src
  79.9 27.0 %encode.2 = (bf16[1024,512]{1,0:T(8,128)(2,1)}, bf16[3,1024,512]{2,1,0:T(8,128)(2,1)}, bf16[8,4,256,256]{3,2,1,0:T(8,128)(2,1)}, bf16[1024,512]{1,0:T(8,128)(2,1...) custom-call(bf16[1024,512]{1,0:T(8,128)(2,1)} %slice_bitcast_fusion.3.sr, ...), custom_call_target="tpu_custom_call" | custom-call | tf_op jit(solution)/shard_map/cond/branch_1_fun/encode/pallas_call | solution.py:455
  106.9 2.3 collective-permute-start
  109.2 34.5 %conditional.8 = ((bf16[1024,512]{1,0:T(8,128)(2,1)}, bf16[3,1024,512]{2,1,0:T(8,128)(2,1)}, bf16[8,4,256,256]{3,2,1,0:T(8,128)(2,1)}, bf16[1024,512]{1,0:T(8,12...) conditional(s32[]{:T(128)} %convert_element_type.15, ...), branch_computations={%region_4.5_spmd, %region_5.6_spmd} | conditional | bytes 4407368 | solution.py:972
  112.8 1.9 slice_bitcast_fusion.13.cols
  114.6 2.3 slice_bitcast_fusion.12.src
  116.9 26.8 %encode.3 = (bf16[1024,512]{1,0:T(8,128)(2,1)}, bf16[3,1024,512]{2,1,0:T(8,128)(2,1)}, bf16[8,4,256,256]{3,2,1,0:T(8,128)(2,1)}, bf16[1024,512]{1,0:T(8,128)(2,1...) custom-call(bf16[1024,512]{1,0:T(8,128)(2,1)} %slice_bitcast_fusion.12.s, ...), custom_call_target="tpu_custom_call" | custom-call | tf_op jit(solution)/shard_map/cond/branch_1_fun/encode/pallas_call | solution.py:455
  143.7 2.3 collective-permute-start.2
  146.0 3.0 pad_maximum_fusion.1
  149.5 18.7 %collective-permute-done.2 = bf16[1024,512]{1,0:T(8,128)(2,1)} collective-permute-done((bf16[1024,512]{1,0:T(8,128)(2,1)}, bf16[1024,512]{1,0:T(8,128)(2,1)}, u32[]{:S(2)}, u32[]{:S(2)}) %collective-permute-start.2) | collective-permute-done | bytes 1048608 | tf_op jit(solution)/shard_map/ppermute | solution.py:920
  171.0 2.4 slice.126
  175.0 1.5 maximum_bitcast_fusion.1
  176.5 100.5 %collective-permute-done.3 = bf16[1024,512]{1,0:T(8,128)(2,1)} collective-permute-done((bf16[1024,512]{1,0:T(8,128)(2,1)}, bf16[1024,512]{1,0:T(8,128)(2,1)}, u32[]{:S(2)}, u32[]{:S(2)}) %collective-permute-start.3) | collective-permute-done | bytes 1048608 | tf_op jit(solution)/shard_map/ppermute | solution.py:920
  277.0 45.0 %conditional.10 = ((f32[1024,512]{1,0:T(8,128)}, bf16[4,512,512]{2,1,0:T(8,128)(2,1)}, bf16[512,2048]{1,0:T(8,128)(2,1)}, bf16[2048,512]{1,0:T(8,128)(2,1)}, bf1...) conditional(s32[]{:T(128)} %convert_element_type.15, (bf16[2,1024,512]{2,1,0:T(8,128)(2,1)}, ...), branch_computations={%region_8.9_spmd, %region_9.10_spmd} | conditional | bytes 4194360 | solution.py:1010
  278.5 2.3 slice_bitcast_fusion.19.refs_0_
  280.8 41.2 %encode_back.2 = (f32[1024,512]{1,0:T(8,128)}, bf16[4,512,512]{2,1,0:T(8,128)(2,1)}, bf16[512,2048]{1,0:T(8,128)(2,1)}, bf16[2048,512]{1,0:T(8,128)(2,1)}, bf16[...) custom-call(bf16[1024,512]{1,0:T(8,128)(2,1)} %slice_bitcast_fusion.19.refs_0_, bf16[1024,512]{1,0:T(8,128)(2,1)} %copy.53.refs_1_, ...), custom_call_target="tpu_custom_call" | custom-call | tf_op jit(solution)/shard_map/cond/branch_1_fun/encode_back/pallas_call | solution.py:455
  322.0 47.9 %conditional.11 = ((f32[1024,512]{1,0:T(8,128)}, bf16[4,512,512]{2,1,0:T(8,128)(2,1)}, bf16[512,2048]{1,0:T(8,128)(2,1)}, bf16[2048,512]{1,0:T(8,128)(2,1)}, bf1...) conditional(s32[]{:T(128)} %convert_element_type.15, (bf16[2,1024,512]{2,1,0:T(8,128)(2,1)}, ...), branch_computations={%region_10.11_spmd, %region_11.12_spmd} | conditional | bytes 8388692 | solution.py:1010
  323.8 2.4 slice_bitcast_fusion.21.refs_0_
  326.2 43.6 %encode_back.3 = (f32[1024,512]{1,0:T(8,128)}, bf16[4,512,512]{2,1,0:T(8,128)(2,1)}, bf16[512,2048]{1,0:T(8,128)(2,1)}, bf16[2048,512]{1,0:T(8,128)(2,1)}, bf16[...) custom-call(bf16[1024,512]{1,0:T(8,128)(2,1)} %slice_bitcast_fusion.21.refs_0_, bf16[1024,512]{1,0:T(8,128)(2,1)} %copy.55.refs_1_, ...), custom_call_target="tpu_custom_call" | custom-call | tf_op jit(solution)/shard_map/cond/branch_1_fun/encode_back/pallas_call | solution.py:455
  370.6 3.3 broadcast_select_fusion.g_down
  373.9 3.3 broadcast_select_fusion.1.g_up
  377.2 1.5 slice_select_fusion
  379.1 1.9 pad_maximum_fusion.g_mats
  381.1 74.9 %scatter.1 = (f32[6,32,512]{2,1,0:T(8,128)}, f32[32,2048]{1,0:T(8,128)}, f32[128,512]{1,0:T(8,128)}, f32[32,1024]{1,0:T(8,128)}, f32[8,512]{1,0:T(8,128)}) custom-call(bf16[6,512,512]{2,1,0:T(8,128)(2,1)} %pad_maximum_fusion.g_mats, bf16[512,2048]{1,0:T(8,128)(2,1)} %broadcast_select_fusion.1.g_up, bf16[2048,512]{1,0:T(8,128)(2,1)} %broadcast_select_fusion.g_down, ...), custom_call_target="tpu_custom_call" | custom-call | tf_op jit(solution)/shard_map/scatter/pallas_call | solution.py:887
  459.2 4.1 maximum_bitcast_fusion
  (76 shorter events, 23.5 us)
Async XLA Ops:
  1.9 68.3 %copy-start.13 = (s32[2,2,1,1024]{3,2,1,0:T(1,128)S(1)}, s32[2,2,1,1024]{3,2,1,0:T(1,128)}, u32[]{:S(2)}) copy-start(s32[2,2,1,1024]{3,2,1,0:T(1,128)} %param.30) | copy-start | bytes 49156
  1.9 68.4 %copy-start.9 = (s32[2,1,1024]{2,1,0:T(1,128)S(1)}, s32[2,1,1024]{2,1,0:T(1,128)}, u32[]{:S(2)}) copy-start(s32[2,1,1024]{2,1,0:T(1,128)} %param.29) | copy-start | bytes 24580
  63.4 7.1 %copy-start.8 = (bf16[768,1024]{1,0:T(8,128)(2,1)S(1)}, bf16[768,1024]{1,0:T(8,128)(2,1)}, u32[]{:S(2)}) copy-start(bf16[768,1024]{1,0:T(8,128)(2,1)} %get-tuple-element.391) | copy-start | bytes 4718596
  65.8 80.1 %collective-permute-start.1 = (bf16[2,512,512]{2,1,0:T(8,128)(2,1)}, bf16[2,512,512]{2,1,0:T(8,128)(2,1)}, u32[]{:S(2)}, u32[]{:S(2)}) collective-permute-start(bf16[2,512,512]{2,1,0:T(8,128)(2,1)} %slice.125), channel_id=1, source_target_pairs={{0,16},{1,17},{2,18},{3,19},{4,20},{5,21},{6,22},{7,23},{8,24},{9,... | collective-permute-start | bytes 3145736 | tf_op jit(solution)/shard_map/ppermute | solution.py:920
  106.9 42.1 %collective-permute-start = (bf16[1024,512]{1,0:T(8,128)(2,1)}, bf16[1024,512]{1,0:T(8,128)(2,1)}, u32[]{:S(2)}, u32[]{:S(2)}) collective-permute-start(bf16[1024,512]{1,0:T(8,128)(2,1)} %get-tuple-element.395), channel_id=1, source_target_pairs={{0,16},{1,17},{2,18},{3,19},{4,20},{5,21},{6,22},{7,23},{8,24},{9,... | collective-permute-start | bytes 3145736 | tf_op jit(solution)/shard_map/ppermute | solution.py:920
  143.7 24.5 %collective-permute-start.2 = (bf16[1024,512]{1,0:T(8,128)(2,1)}, bf16[1024,512]{1,0:T(8,128)(2,1)}, u32[]{:S(2)}, u32[]{:S(2)}) collective-permute-start(bf16[1024,512]{1,0:T(8,128)(2,1)} %get-tuple-element.398), channel_id=1, source_target_pairs={{0,16},{1,17},{2,18},{3,19},{4,20},{5,21},{6,22},{7,23},{8,24},{9,... | collective-permute-start | bytes 3145736 | tf_op jit(solution)/shard_map/ppermute | solution.py:920
  168.4 108.6 %collective-permute-start.3 = (bf16[1024,512]{1,0:T(8,128)(2,1)}, bf16[1024,512]{1,0:T(8,128)(2,1)}, u32[]{:S(2)}, u32[]{:S(2)}) collective-permute-start(bf16[1024,512]{1,0:T(8,128)(2,1)} %get-tuple-element.416), channel_id=1, source_target_pairs={{16,0},{17,1},{18,2},{19,3},{20,4},{21,5},{22,6},{23,7},{24,8},{25... | collective-permute-start | bytes 3145736 | tf_op jit(solution)/shard_map/ppermute | solution.py:920
  169.7 152.3 %collective-permute-start.4 = (bf16[1024,512]{1,0:T(8,128)(2,1)}, bf16[1024,512]{1,0:T(8,128)(2,1)}, u32[]{:S(2)}, u32[]{:S(2)}) collective-permute-start(bf16[1024,512]{1,0:T(8,128)(2,1)} %get-tuple-element.423), channel_id=1, source_target_pairs={{16,0},{17,1},{18,2},{19,3},{20,4},{21,5},{22,6},{23,7},{24,8},{25... | collective-permute-start | bytes 3145736 | tf_op jit(solution)/shard_map/ppermute | solution.py:920
  171.0 3.7 copy-start.2
  171.0 3.7 copy-start.3
  173.4 203.8 %collective-permute-start.5 = (bf16[2,512,512]{2,1,0:T(8,128)(2,1)}, bf16[2,512,512]{2,1,0:T(8,128)(2,1)}, u32[]{:S(2)}, u32[]{:S(2)}) collective-permute-start(bf16[2,512,512]{2,1,0:T(8,128)(2,1)} %slice.126), channel_id=1, source_target_pairs={{16,0},{17,1},{18,2},{19,3},{20,4},{21,5},{22,6},{23,7},{24,8},{25... | collective-permute-start | bytes 3145736 | tf_op jit(solution)/shard_map/ppermute | solution.py:920
  323.8 2.4 copy-start.1
  370.6 3.3 copy-start.5
  373.9 3.3 copy-start.6
  377.2 1.9 copy-start.4
  381.1 78.2 %copy-start.7 = (f32[1024,512]{1,0:T(8,128)S(1)}, f32[1024,512]{1,0:T(8,128)}, u32[]{:S(2)}) copy-start(f32[1024,512]{1,0:T(8,128)} %get-tuple-element.427) | copy-start | bytes 6291460
  459.2 5.5 %copy-start.12 = (f32[32,1024]{1,0:T(8,128)S(1)}, f32[32,1024]{1,0:T(8,128)}, u32[]{:S(2)}) copy-start(f32[32,1024]{1,0:T(8,128)} %get-tuple-element.437) | copy-start | bytes 393220
  459.2 6.2 %copy-start.11 = (f32[32,2048]{1,0:T(8,128)S(1)}, f32[32,2048]{1,0:T(8,128)}, u32[]{:S(2)}) copy-start(f32[32,2048]{1,0:T(8,128)} %get-tuple-element.439) | copy-start | bytes 786436
  459.2 6.9 %copy-start.10 = (f32[128,512]{1,0:T(8,128)S(1)}, f32[128,512]{1,0:T(8,128)}, u32[]{:S(2)}) copy-start(f32[128,512]{1,0:T(8,128)} %get-tuple-element.440) | copy-start | bytes 786436
